TPU v7x, 32 devices: a whole 2x2x4 slice. The times are simulated.
32 devices in a mesh: dp: 8 (over y, x, core), fsdp: 4 (over z).
Axes of the slice: x: 2, y: 2, z: 4, core: 2. Of those that a mesh axis runs over, the one named last changes fastest.
Arguments:
- tokens: bfloat16 [16384, 768], P(('dp', 'fsdp')), may hold values from -6 to 6
- doc_ids: int32 [16384], P(('dp', 'fsdp')), may hold values from 0 to 127, as said below
- pass_embed: bfloat16 [768], P(('dp', 'fsdp')), may hold values from -6 to 6
- ln1_gain: bfloat16 [768], P(('dp', 'fsdp')), may hold values from 0.5 to 1.5
- w_qkv: bfloat16 [768, 2304], P(('dp', 'fsdp')), may hold values from -0.21875 to 0.21875
- w_out: bfloat16 [768, 768], P(('dp', 'fsdp')), may hold values from -0.75 to 0.75
- ln2_gain: bfloat16 [768], P(('dp', 'fsdp')), may hold values from 0.5 to 1.5
- w_up: bfloat16 [768, 3072], P(('dp', 'fsdp')), may hold values from -0.21875 to 0.21875
- w_down: bfloat16 [3072, 768], P(('dp', 'fsdp')), may hold values from -0.109375 to 0.109375
- cotangent: bfloat16 [16384, 768], P(('dp', 'fsdp')), may hold values from -6 to 6
Outputs:
- layer_out: bfloat16 [16384, 768], P(('dp', 'fsdp'))
- tokens_grad: float32 [16384, 768], P(('dp', 'fsdp'))
- embed_grad: float32 [768], P(('dp', 'fsdp'))
- ln1_grad: float32 [768], P(('dp', 'fsdp'))
- qkv_grad: float32 [768, 2304], P(('dp', 'fsdp'))
- wout_grad: float32 [768, 768], P(('dp', 'fsdp'))
- ln2_grad: float32 [768], P(('dp', 'fsdp'))
- up_grad: float32 [768, 3072], P(('dp', 'fsdp'))
- down_grad: float32 [3072, 768], P(('dp', 'fsdp'))
Inputs may be any that keep to these rules, and one draw needn't show every extreme that they name: `doc_ids`: the tokens of one device, 512 in a row from a multiple of 512, form 1, 2 or 4 documents of equal length, numbered 4 b to 4 b + 3 within the b-th such block; the first block holds one document and the last four.
All inputs are finite; a program needn't handle non-finite values.
Results may differ from a plain program's by a relative error of at most 0.014.
Values may be sent and summed in bfloat16 or wider, within the bound.
A program may use at most 256 MiB of HBM per device.

v0:
```python
import jax
import jax.numpy as jnp
from jax import lax
from jax.sharding import PartitionSpec as P

HEAD_DIM = 64


EPS = 1e-05


def layer_norm(values, gain):
    center = values - jnp.mean(values, -1, keepdims=True)
    spread = jnp.mean(center * center, -1, keepdims=True)
    return center * lax.rsqrt(spread + EPS) * gain


def exact_gelu(values):
    return jax.nn.gelu(values, approximate=False)


def regather(shards):
    return (
        lax.all_gather(shards[0], ("dp", "fsdp"), axis=0, tiled=True),
        lax.all_gather(shards[1], ("dp", "fsdp"), axis=0, tiled=True),
        lax.all_gather(shards[2], ("dp", "fsdp"), axis=0, tiled=True),
        lax.all_gather(shards[3], ("dp", "fsdp"), axis=0, tiled=True),
        lax.all_gather(shards[4], ("dp", "fsdp"), axis=0, tiled=True),
        lax.all_gather(shards[5], ("dp", "fsdp"), axis=0, tiled=True),
        lax.all_gather(shards[6], ("dp", "fsdp"), axis=0, tiled=True),
    )


def run_block(inputs, earlier, allowed, weights):
    embed, ln1_w, qkv_w, out_w, ln2_w, up_w, down_w = weights
    length, model_width = inputs.shape
    head_count = model_width // HEAD_DIM
    scale = HEAD_DIM ** (-0.5)
    normed = layer_norm(inputs, ln1_w.astype(jnp.float32)).astype(jnp.bfloat16)
    qkv = jnp.dot(normed, qkv_w, preferred_element_type=jnp.float32).astype(jnp.bfloat16)
    qkv = qkv.reshape(length, 3, head_count, HEAD_DIM)
    queries, own_keys, own_values = (qkv[:, 0], qkv[:, 1], qkv[:, 2])
    if earlier is None:
        key_rows, value_rows = (own_keys, own_values)
    else:
        key_rows = jnp.concatenate([earlier[0], own_keys], 0)
        value_rows = jnp.concatenate([earlier[1], own_values], 0)
    scores = (
        jnp.einsum("qhd,khd->hqk", queries, key_rows, preferred_element_type=jnp.float32) * scale
    )
    scores = jnp.where(allowed[None], scores, -1e30)
    peak = jnp.max(scores, -1, keepdims=True)
    expos = jnp.exp(scores - peak)
    probs = expos / jnp.sum(expos, -1, keepdims=True)
    attn = jnp.einsum(
        "hqk,khd->qhd", probs.astype(jnp.bfloat16), value_rows, preferred_element_type=jnp.float32
    )
    attn = attn.astype(jnp.bfloat16).reshape(length, model_width)
    middle = inputs + jnp.dot(attn, out_w, preferred_element_type=jnp.float32)
    second = layer_norm(middle, ln2_w.astype(jnp.float32)).astype(jnp.bfloat16)
    hidden = jnp.dot(second, up_w, preferred_element_type=jnp.float32)
    active = exact_gelu(hidden).astype(jnp.bfloat16)
    result = middle + jnp.dot(active, down_w, preferred_element_type=jnp.float32)
    kept = {
        "normed": normed,
        "queries": queries,
        "key_rows": key_rows,
        "value_rows": value_rows,
        "probs": probs,
        "attn": attn,
        "middle": middle,
        "second": second,
        "hidden": hidden,
        "active": active,
        "own_kv": (own_keys, own_values),
    }
    return (result, kept)


def run_back(inputs, earlier, allowed, weights, upstream, extra):
    embed, ln1_w, qkv_w, out_w, ln2_w, up_w, down_w = weights
    length, model_width = inputs.shape
    head_count = model_width // HEAD_DIM
    scale = HEAD_DIM ** (-0.5)
    unused, kept = run_block(inputs, earlier, allowed, weights)
    down_rounded = upstream.astype(jnp.bfloat16)
    down_g = jnp.dot(kept["active"].T, down_rounded, preferred_element_type=jnp.float32)
    active_g = jnp.dot(down_rounded, down_w.T, preferred_element_type=jnp.float32)
    unused_gelu, gelu_pull = jax.vjp(exact_gelu, kept["hidden"])
    hidden_g = gelu_pull(active_g)[0].astype(jnp.bfloat16)
    up_g = jnp.dot(kept["second"].T, hidden_g, preferred_element_type=jnp.float32)
    second_g = jnp.dot(hidden_g, up_w.T, preferred_element_type=jnp.float32)
    unused_norm, norm_pull = jax.vjp(layer_norm, kept["middle"], ln2_w.astype(jnp.float32))
    middle_part, ln2_g = norm_pull(second_g)
    middle_g = upstream + middle_part
    attn_rounded = middle_g.astype(jnp.bfloat16)
    wout_g = jnp.dot(kept["attn"].T, attn_rounded, preferred_element_type=jnp.float32)
    attn_g = jnp.dot(attn_rounded, out_w.T, preferred_element_type=jnp.float32)
    attn_g = attn_g.astype(jnp.bfloat16).reshape(length, head_count, HEAD_DIM)
    probs = kept["probs"]
    value_g = jnp.einsum(
        "hqk,qhd->khd", probs.astype(jnp.bfloat16), attn_g, preferred_element_type=jnp.float32
    )
    probs_g = jnp.einsum(
        "qhd,khd->hqk", attn_g, kept["value_rows"], preferred_element_type=jnp.float32
    )
    scores_g = probs * (probs_g - jnp.sum(probs * probs_g, -1, keepdims=True))
    scores_g = scores_g.astype(jnp.bfloat16)
    query_g = (
        jnp.einsum("hqk,khd->qhd", scores_g, kept["key_rows"], preferred_element_type=jnp.float32)
        * scale
    )
    key_g = (
        jnp.einsum("hqk,qhd->khd", scores_g, kept["queries"], preferred_element_type=jnp.float32)
        * scale
    )
    if earlier is None:
        earlier_g = None
        own_key_g, own_value_g = (key_g, value_g)
    else:
        earlier_g = (key_g[:length], value_g[:length])
        own_key_g, own_value_g = (key_g[length:], value_g[length:])
    if extra is not None:
        own_key_g = own_key_g + extra[0]
        own_value_g = own_value_g + extra[1]
    qkv_rounded = jnp.stack([query_g, own_key_g, own_value_g], 1).astype(jnp.bfloat16)
    qkv_rounded = qkv_rounded.reshape(length, 3 * model_width)
    qkv_g = jnp.dot(kept["normed"].T, qkv_rounded, preferred_element_type=jnp.float32)
    normed_g = jnp.dot(qkv_rounded, qkv_w.T, preferred_element_type=jnp.float32)
    unused_first, first_pull = jax.vjp(layer_norm, inputs, ln1_w.astype(jnp.float32))
    input_part, ln1_g = first_pull(normed_g)
    input_g = middle_g + input_part
    return ((ln1_g, qkv_g, wout_g, ln2_g, up_g, down_g), input_g, earlier_g)


def body(tokens, doc_ids, pass_embed, ln1_gain, w_qkv, w_out, ln2_gain, w_up, w_down, cotangent):
    shards = (pass_embed, ln1_gain, w_qkv, w_out, ln2_gain, w_up, w_down)
    weights = (
        lax.all_gather(shards[0], ("dp", "fsdp"), axis=0, tiled=True),
        lax.all_gather(shards[1], ("dp", "fsdp"), axis=0, tiled=True),
        lax.all_gather(shards[2], ("dp", "fsdp"), axis=0, tiled=True),
        lax.all_gather(shards[3], ("dp", "fsdp"), axis=0, tiled=True),
        lax.all_gather(shards[4], ("dp", "fsdp"), axis=0, tiled=True),
        lax.all_gather(shards[5], ("dp", "fsdp"), axis=0, tiled=True),
        lax.all_gather(shards[6], ("dp", "fsdp"), axis=0, tiled=True),
    )
    length = tokens.shape[0]
    places = jnp.arange(length, dtype=jnp.int32)
    allowed = (doc_ids[:, None] == doc_ids[None, :]) & (places[None, :] <= places[:, None])
    doubled = jnp.concatenate([allowed, allowed], 1)
    inputs = tokens.astype(jnp.float32)
    first_out, first_kept = run_block(inputs, None, allowed, weights)
    earlier = first_kept["own_kv"]
    weights = regather(shards)
    second_in = first_out + weights[0].astype(jnp.float32)
    second_out, unused = run_block(second_in, earlier, doubled, weights)
    layer_out = second_out.astype(jnp.bfloat16)
    weights = regather(shards)
    late_grads, second_in_g, earlier_g = run_back(
        second_in, earlier, doubled, weights, cotangent.astype(jnp.float32), None
    )
    embed_g = jnp.sum(second_in_g, 0)
    early_grads, tokens_grad, unused_g = run_back(
        inputs, None, allowed, weights, second_in_g, earlier_g
    )
    totals = (embed_g,) + tuple((a + b for a, b in zip(late_grads, early_grads)))
    summed = lax.psum_scatter(totals, ("dp", "fsdp"), scatter_dimension=0, tiled=True)
    return (
        layer_out,
        tokens_grad,
        summed[0],
        summed[1],
        summed[2],
        summed[3],
        summed[4],
        summed[5],
        summed[6],
    )


def solution(mesh):
    placed = (
        P(("dp", "fsdp"), None),
        P(("dp", "fsdp")),
        P(("dp", "fsdp")),
        P(("dp", "fsdp")),
        P(("dp", "fsdp"), None),
        P(("dp", "fsdp"), None),
        P(("dp", "fsdp")),
        P(("dp", "fsdp"), None),
        P(("dp", "fsdp"), None),
        P(("dp", "fsdp"), None),
    )
    return jax.shard_map(
        body,
        mesh=mesh,
        in_specs=placed,
        out_specs=(
            P(("dp", "fsdp"), None),
            P(("dp", "fsdp"), None),
            P(("dp", "fsdp")),
            P(("dp", "fsdp")),
            P(("dp", "fsdp"), None),
            P(("dp", "fsdp"), None),
            P(("dp", "fsdp")),
            P(("dp", "fsdp"), None),
            P(("dp", "fsdp"), None),
        ),
        check_vma=False,
    )
```

profile of v0, /device:TPU:0, one launch (start us, length us, event | category | flops | bytes accessed | tf_op | source)
XLA Modules:
  0.0 999.4 jit_solution(14728418093591067328)
XLA Ops:
  12.6 42.2 %all-reduce.7 = (bf16[768]{0:T(1024)(128)(2,1)S(1)}, bf16[768]{0:T(1024)(128)(2,1)S(1)}, bf16[768]{0:T(1024)(128)(2,1)S(1)}) all-reduce(bf16[768]{0:T(1024)(128)(2,1)S(1)} %dynamic-update-slice, bf16[768]{0:T(1024)(128)(2,1)S(1)} %dynamic-update-slice.1, ...), channel_id=1, replica_groups=mesh['dp'=8,'fsdp'=4] {'dp','fsdp'}, use_global_device_ids=true, to_apply=%add | all-reduce | flops 2304 | bytes 9216
  55.9 1.5 copy.44
  57.4 1.3 convert_reduce_fusion
  59.2 14.6 %all-gather.5.cloned.1.call-done = bf16[768,2304]{1,0:T(8,128)(2,1)} async-done(((bf16[24,2304]{1,0:T(8,128)(2,1)}), bf16[768,2304]{1,0:T(8,128)(2,1)}) %all-gather.5.cloned.1.call-update) | async-done | bytes 3538960 | tf_op jit(solution)/shard_map/all_gather | solution.py:141
  73.8 5.5 convolution_convert_fusion.1
  79.4 2.8 copy.41
  82.2 7.6 fusion.101
  89.8 6.7 fusion.47
  96.5 33.0 %all-gather.7.cloned.1.call-done = bf16[768,768]{1,0:T(8,128)(2,1)} async-done(((bf16[24,768]{1,0:T(8,128)(2,1)}), bf16[768,768]{1,0:T(8,128)(2,1)}) %all-gather.7.cloned.1.call-update) | async-done | bytes 1179664 | tf_op jit(solution)/shard_map/all_gather | solution.py:142
  129.5 2.4 fusion.102
  132.3 62.6 %all-gather.9.cloned.1.call-done = bf16[768,3072]{1,0:T(8,128)(2,1)} async-done(((bf16[24,3072]{1,0:T(8,128)(2,1)}), bf16[768,3072]{1,0:T(8,128)(2,1)}) %all-gather.9.cloned.1.call-update) | async-done | bytes 4718608 | tf_op jit(solution)/shard_map/all_gather | solution.py:144
  194.8 20.0 %multiply_convert_fusion.3 = (bf16[512,3072]{1,0:T(8,128)(2,1)}, f32[512,3072]{1,0:T(8,128)}, f32[512,3072]{1,0:T(8,128)}) fusion(bf16[768,3072]{1,0:T(8,128)(2,1)} %all-gather.9.cloned.1.call-done, f32[512,768]{1,0:T(8,128)S(1)} %get-tuple-element.42, f32[768]{0:T(1024)S(1)} %convert_element_type.129, f32[512]{0:T(512)S(1)} %fusion.76, ...), kind=kOutput, calls=%fused_computation.39 | convolution fusion | flops 2519728128 | bytes 22027264 | tf_op jit(solution)/shard_map/dot_general | solution.py:61
  214.8 45.1 %all-gather.11.cloned.1.call-done = bf16[3072,768]{1,0:T(8,128)(2,1)} async-done(((bf16[96,768]{1,0:T(8,128)(2,1)}), bf16[3072,768]{1,0:T(8,128)(2,1)}) %all-gather.11.cloned.1.call-update) | async-done | bytes 4718608 | tf_op jit(solution)/shard_map/all_gather | solution.py:145
  259.9 6.1 fusion.103
  266.4 3.5 convolution_convert_fusion
  269.9 4.3 copy.43
  274.2 2.2 slice_bitcast_fusion
  277.5 10.1 %fusion.62 = f32[12,512,1024]{2,1,0:T(8,128)} fusion(bf16[512,12,64]{0,2,1:T(8,128)(2,1)S(1)} %get-tuple-element.37, bf16[512,12,64]{0,2,1:T(8,128)(2,1)S(1)} %get-tuple-element.60, bf16[512,3,12,64]{0,3,2,1:T(8,128)(2,1)S(1)} %bitcast.124), kind=kOutput, calls=%fused_computation.130 | convolution fusion | flops 808452096 | bytes 27525120 | tf_op jit(solution)/shard_map/qhd,khd->hqk/dot_general | solution.py:49
  287.6 33.8 %fusion.104 = (f32[12,512]{1,0:T(8,128)S(1)}, f32[12,512,1024]{2,1,0:T(8,128)}) fusion(f32[12,512,1024]{2,1,0:T(8,128)} %fusion.62, pred[512,1024]{1,0:T(8,128)(4,1)} %copy.44), kind=kOutput, calls=%fused_computation.188 | output fusion | flops 37749760 | bytes 50880512 | tf_op jit(solution)/shard_map/sub | solution.py:53
  321.5 10.4 %fusion.50 = bf16[12,64,512]{2,1,0:T(8,128)(2,1)S(1)} fusion(bf16[512,12,64]{0,2,1:T(8,128)(2,1)S(1)} %get-tuple-element.38, bf16[512,12,64]{0,2,1:T(8,128)(2,1)S(1)} %get-tuple-element.59, f32[12,512,1024]{2,1,0:T(8,128)} %get-tuple-element.47, f32[12,512]{1,0:T(8,128)S(1)} %get-tuple-element.46), kind=kOutput, calls=%fused_computation.122 | convolution fusion | flops 821428224 | bytes 27549696 | tf_op jit(solution)/shard_map/hqk,khd->qhd/dot_general | solution.py:55
  333.2 5.5 fusion.94
  338.8 18.2 %add_convert_fusion.1 = (bf16[512,3072]{1,0:T(8,128)(2,1)S(1)}, f32[512,3072]{1,0:T(8,128)}) fusion(f32[512,3072]{1,0:T(8,128)S(1)} %fusion.94, bf16[512,768]{1,0:T(8,128)(2,1)S(1)} %copy-done.36, bf16[3072,768]{1,0:T(8,128)(2,1)S(1)} %bitcast.146), kind=kOutput, calls=%fused_computation.21 | convolution fusion | flops 2529165312 | bytes 21233664 | tf_op jit(solution)/shard_map/dot_general | solution.py:88
  357.0 3.4 multiply_reduce_fusion.3
  361.1 1.2 copy-done.17
  363.4 1.2 copy.45
  364.6 11.6 %fusion.34 = f32[1024,12,64]{0,2,1:T(8,128)} fusion(bf16[512,12,64]{0,2,1:T(8,128)(2,1)} %bitcast.143, f32[12,512,1024]{2,1,0:T(8,128)} %get-tuple-element.47, f32[12,512]{1,0:T(8,128)S(1)} %get-tuple-element.46), kind=kOutput, calls=%fused_computation.82 | convolution fusion | flops 817889280 | bytes 29122560 | tf_op jit(solution)/shard_map/hqk,qhd->khd/dot_general | solution.py:101
  376.2 16.4 %multiply_reduce_fusion = (f32[12,512]{1,0:T(8,128)S(1)}, f32[12,512,1024]{2,1,0:T(8,128)}) fusion(f32[12,512,1024]{2,1,0:T(8,128)} %get-tuple-element.47, f32[12,512]{1,0:T(8,128)S(1)} %get-tuple-element.46, bf16[512,12,64]{0,2,1:T(8,128)(2,1)} %bitcast.144, bf16[512,12,64]{0,2,1:T(8,128)(2,1)S(1)} %get-tuple-element.38, bf16[512,12,64]{0,2,1:T(8,128)(2,1)S(1)} %copy-done.44), kind=kOutput, calls=%fused_computation.3 | convolution fusion | flops 827320320 | bytes 52740096 | tf_op jit(solution)/shard_map/qhd,khd->hqk/dot_general | solution.py:104
  392.6 16.7 %multiply_convert_fusion = bf16[12,512,1024]{2,1,0:T(8,128)(2,1)S(1)} fusion(f32[12,512,1024]{2,1,0:T(8,128)} %get-tuple-element.52, f32[12,512]{1,0:T(8,128)S(1)} %get-tuple-element.51, f32[12,512,1024]{2,1,0:T(8,128)} %get-tuple-element.47, f32[12,512]{1,0:T(8,128)S(1)} %get-tuple-element.46), kind=kLoop, calls=%fused_computation.2 | loop fusion | flops 25165824 | bytes 62963712 | tf_op jit(solution)/shard_map/convert_element_type | solution.py:108
  409.3 4.5 copy-done
  413.8 3.6 multiply_bitcast_fusion
  417.5 9.7 fusion.55
  427.1 2.2 fusion.106
  429.3 1.5 fusion.66
  432.3 2.0 copy-done.76
  434.3 2.4 multiply_reduce_fusion.4
  438.6 7.9 add_convert_fusion
  446.6 6.4 multiply_reduce_fusion.2
  453.9 1.2 copy-done.15
  455.1 1.7 convolution_convert_fusion.2
  456.8 1.4 copy.46
  458.2 10.5 %multiply_reduce_fusion.1 = (f32[12,512]{1,0:T(8,128)S(1)}, f32[12,512,512]{1,2,0:T(8,128)}) fusion(f32[12,512,512]{1,2,0:T(8,128)} %get-tuple-element.40, f32[12,512]{1,0:T(8,128)S(1)} %copy-done.65, bf16[512,12,64]{0,2,1:T(8,128)(2,1)S(1)} %bitcast.141, bf16[512,3,12,64]{0,3,2,1:T(8,128)(2,1)} %bitcast.128), kind=kOutput, calls=%fused_computation.8 | convolution fusion | flops 412084224 | bytes 26787840 | tf_op jit(solution)/shard_map/qhd,khd->hqk/dot_general | solution.py:104
  468.8 1.3 slice-done.1
  470.1 1.2 slice-done.2
  471.3 6.9 multiply_convert_fusion.1
  478.3 3.9 fusion.57
  483.1 2.2 convolution_add_fusion.3
  485.6 4.3 fusion.56
  489.9 6.8 fusion.58
  497.0 1.4 copy-done.23
  498.4 2.3 fusion.92
  500.8 5.3 convolution_add_fusion
  506.2 1.3 copy-done.7
  507.5 4.9 fusion.93
  512.5 5.7 convolution_add_fusion.2
  518.5 6.2 multiply_convert_fusion.2
  524.7 2.7 fusion.107
  528.2 5.3 convolution_add_fusion.1
  533.6 5.0 fusion.42
  540.5 40.3 %all-reduce.6 = (f32[768]{0:T(1024)S(1)}, f32[768]{0:T(1024)S(1)}, f32[768]{0:T(1024)S(1)}) all-reduce(f32[768]{0:T(1024)S(1)} %get-tuple-element.23, f32[768]{0:T(1024)S(1)} %add.136, f32[768]{0:T(1024)S(1)} %add.139), channel_id=2, replica_groups=mesh['dp'=8,'fsdp'=4] {'dp','fsdp'}, use_global_device_ids=true, to_apply=%region_23.24.clone | all-reduce | flops 2304 | bytes 18432
  582.5 3.6 add_add_fusion.4
  586.1 5.8 add_convert_fusion.2
  591.9 116.7 %reduce-scatter.5.cloned.1.call-done = f32[24,2304]{1,0:T(8,128)} async-done(((f32[768,2304]{1,0:T(8,128)}), f32[24,2304]{1,0:T(8,128)}) %reduce-scatter.5.cloned.1.call-update) | async-done | bytes 221200 | tf_op jit(solution)/shard_map/reduce_scatter | solution.py:167
  708.6 141.2 %reduce-scatter.9.cloned.1.call-done = f32[24,3072]{1,0:T(8,128)} async-done(((f32[768,3072]{1,0:T(8,128)}), f32[24,3072]{1,0:T(8,128)}) %reduce-scatter.9.cloned.1.call-update) | async-done | bytes 294928 | tf_op jit(solution)/shard_map/reduce_scatter | solution.py:167
  849.8 142.2 %reduce-scatter.11.cloned.1.call-done = f32[96,768]{1,0:T(8,128)} async-done(((f32[3072,768]{1,0:T(8,128)}), f32[96,768]{1,0:T(8,128)}) %reduce-scatter.11.cloned.1.call-update) | async-done | bytes 294928 | tf_op jit(solution)/shard_map/reduce_scatter | solution.py:167
  (233 shorter events, 21.9 us)
Async XLA Ops:
  7.2 51.6 %copy-start.2 = (bf16[512,768]{1,0:T(8,128)(2,1)S(1)}, bf16[512,768]{1,0:T(8,128)(2,1)}, u32[]{:S(2)}) copy-start(bf16[512,768]{1,0:T(8,128)(2,1)} %param.10) | copy-start | bytes 2359300
  7.2 66.6 %all-gather.5.cloned.1.call-start = ((), (), s32[]{:S(2)}) async-start(), calls=%async_computation.4 | async-start | bytes 3649536 | tf_op jit(solution)/shard_map/all_gather | solution.py:141
  7.9 121.6 %all-gather.7.cloned.1.call-start = ((), (), s32[]{:S(2)}) async-start(), calls=%async_computation.5 | async-start | bytes 1216512 | tf_op jit(solution)/shard_map/all_gather | solution.py:142
  8.7 186.2 %all-gather.9.cloned.1.call-start = ((), (), s32[]{:S(2)}) async-start(), calls=%async_computation.6 | async-start | bytes 4866048 | tf_op jit(solution)/shard_map/all_gather | solution.py:144
  9.4 250.5 %all-gather.11.cloned.1.call-start = ((), (), s32[]{:S(2)}) async-start(), calls=%async_computation.7 | async-start | bytes 4866048 | tf_op jit(solution)/shard_map/all_gather | solution.py:145
  10.0 582.0 %reduce-scatter.7.cloned.1.call-start = ((), (), s32[]{:S(2)}) async-start(), calls=%async_computation.9 | async-start | bytes 2433024 | tf_op jit(solution)/shard_map/reduce_scatter | solution.py:167
  54.8 211.6 %copy-start.47 = (f32[768]{0:T(1024)}, f32[768]{0:T(1024)S(1)}, u32[]{:S(2)}) copy-start(f32[768]{0:T(1024)S(1)} %convert_element_type.123) | copy-start | bytes 9220
  58.8 15.0 %copy-start.52 = (f32[512]{0:T(512)}, f32[512]{0:T(512)S(1)}, u32[]{:S(2)}) copy-start(f32[512]{0:T(512)S(1)} %broadcast_multiply_fusion.3) | copy-start | bytes 6148
  59.1 14.7 %copy-start.68 = (f32[512]{0:T(512)}, f32[512]{0:T(512)S(1)}, u32[]{:S(2)}) copy-start(f32[512]{0:T(512)S(1)} %fusion.41) | copy-start | bytes 6148
  59.2 14.7 %copy-start.58 = (f32[512]{0:T(512)}, f32[512]{0:T(512)S(1)}, u32[]{:S(2)}) copy-start(f32[512]{0:T(512)S(1)} %fusion.75) | copy-start | bytes 6148
  82.2 7.6 copy-start.12
  89.8 6.7 copy-start.64
  131.9 128.0 %copy-start.9 = (f32[512,768]{1,0:T(8,128)}, f32[512,768]{1,0:T(8,128)S(1)}, u32[]{:S(2)}) copy-start(f32[512,768]{1,0:T(8,128)S(1)} %get-tuple-element.42) | copy-start | bytes 4718596
  131.9 82.9 %copy-start.60 = (f32[512]{0:T(512)}, f32[512]{0:T(512)S(1)}, u32[]{:S(2)}) copy-start(f32[512]{0:T(512)S(1)} %broadcast_multiply_fusion.2) | copy-start | bytes 6148
  132.3 82.6 %copy-start.70 = (f32[512]{0:T(512)}, f32[512]{0:T(512)S(1)}, u32[]{:S(2)}) copy-start(f32[512]{0:T(512)S(1)} %multiply_reduce_fusion.10) | copy-start | bytes 6148
  132.3 82.5 %copy-start.66 = (f32[512]{0:T(512)}, f32[512]{0:T(512)S(1)}, u32[]{:S(2)}) copy-start(f32[512]{0:T(512)S(1)} %fusion.76) | copy-start | bytes 6148
  259.9 6.5 copy-start.75
  266.0 65.9 %copy-start.4 = (f32[512,768]{1,0:T(8,128)}, f32[512,768]{1,0:T(8,128)S(1)}, u32[]{:S(2)}) copy-start(f32[512,768]{1,0:T(8,128)S(1)} %get-tuple-element.45) | copy-start | bytes 4718596
  266.0 3.9 copy-start.54
  276.4 45.0 %copy-start.43 = (bf16[512,12,64]{0,2,1:T(8,128)(2,1)}, bf16[512,12,64]{0,2,1:T(8,128)(2,1)S(1)}, u32[]{:S(2)}) copy-start(bf16[512,12,64]{0,2,1:T(8,128)(2,1)S(1)} %get-tuple-element.59) | copy-start | bytes 2359300
  321.5 10.4 %copy-start.40 = (bf16[768,768]{1,0:T(8,128)(2,1)S(1)}, bf16[768,768]{1,0:T(8,128)(2,1)}, u32[]{:S(2)}) copy-start(bf16[768,768]{1,0:T(8,128)(2,1)} %all-gather.7.cloned.1.call-done) | copy-start | bytes 3538948
  331.9 6.9 slice-start.3
  332.8 27.6 %copy-start.6 = (f32[512,768]{1,0:T(8,128)}, f32[512,768]{1,0:T(8,128)S(1)}, u32[]{:S(2)}) copy-start(f32[512,768]{1,0:T(8,128)S(1)} %get-tuple-element.49) | copy-start | bytes 4718596
  332.8 27.6 %copy-start.50 = (f32[512]{0:T(512)}, f32[512]{0:T(512)S(1)}, u32[]{:S(2)}) copy-start(f32[512]{0:T(512)S(1)} %broadcast_multiply_fusion) | copy-start | bytes 6148
  333.2 27.3 %copy-start.56 = (f32[512]{0:T(512)}, f32[512]{0:T(512)S(1)}, u32[]{:S(2)}) copy-start(f32[512]{0:T(512)S(1)} %fusion.78) | copy-start | bytes 6148
  333.2 5.6 copy-start.36
  333.2 5.6 slice-start.4
  333.2 23.8 %slice-start.7 = ((s8[4718592]{0:T(1024)(128)(4,1)}), s8[4194304]{0:T(1024)(128)(4,1)S(1)}, s32[]{:S(2)}) async-start(s8[4718592]{0:T(1024)(128)(4,1)} %bitcast.149), calls=%async_computation.19 | async-start | bytes 8388608
  338.8 18.2 %copy-start.31 = (f32[512,3072]{1,0:T(8,128)}, f32[512,3072]{1,0:T(8,128)S(1)}, u32[]{:S(2)}) copy-start(f32[512,3072]{1,0:T(8,128)S(1)} %fusion.94) | copy-start | bytes 18874372
  338.8 18.2 %slice-start.8 = ((s8[4718592]{0:T(1024)(128)(4,1)}), s8[524288]{0:T(1024)(128)(4,1)S(1)}, s32[]{:S(2)}) async-start(s8[4718592]{0:T(1024)(128)(4,1)} %bitcast.149), calls=%async_computation.20 | async-start | bytes 1048576
  364.6 11.6 %copy-start.44 = (bf16[512,12,64]{0,2,1:T(8,128)(2,1)S(1)}, bf16[512,12,64]{0,2,1:T(8,128)(2,1)}, u32[]{:S(2)}) copy-start(bf16[512,12,64]{0,2,1:T(8,128)(2,1)} %copy-done.43) | copy-start | bytes 2359300
  409.3 4.5 copy-start
  413.8 3.6 copy-start.26
  413.8 3.6 copy-start.28
  417.4 13.4 %copy-start.19 = (f32[1024,12,64]{0,2,1:T(8,128)}, f32[1024,12,64]{0,2,1:T(8,128)S(1)}, u32[]{:S(2)}) copy-start(f32[1024,12,64]{0,2,1:T(8,128)S(1)} %multiply_bitcast_fusion) | copy-start | bytes 9437188
  417.4 9.7 copy-start.35
  431.0 7.5 slice-start.5
  431.3 5.4 copy-start.22
  434.3 4.3 slice-start.6
  438.5 15.1 %copy-start.13 = (f32[512,768]{1,0:T(8,128)}, f32[512,768]{1,0:T(8,128)S(1)}, u32[]{:S(2)}) copy-start(f32[512,768]{1,0:T(8,128)S(1)} %get-tuple-element.24) | copy-start | bytes 4718596
  438.6 7.9 copy-start.10
  438.6 7.9 copy-start.61
  438.6 7.9 copy-start.67
  446.5 6.4 copy-start.32
  446.5 6.4 copy-start.71
  458.2 10.6 %copy-start.45 = (bf16[512,768]{0,1:T(8,128)(2,1)}, bf16[512,768]{0,1:T(8,128)(2,1)S(1)}, u32[]{:S(2)}) copy-start(bf16[512,768]{0,1:T(8,128)(2,1)S(1)} %copy.46) | copy-start | bytes 2359300
  458.2 10.6 %slice-start = ((s8[12582912]{0:T(1024)(128)(4,1)}), s8[4194304]{0:T(1024)(128)(4,1)S(1)}, s32[]{:S(2)}) async-start(s8[12582912]{0:T(1024)(128)(4,1)} %bitcast.131), calls=%async_computation.12 | async-start | bytes 8388608
  458.2 11.9 %slice-start.1 = ((s8[12582912]{0:T(1024)(128)(4,1)}), s8[4194304]{0:T(1024)(128)(4,1)S(1)}, s32[]{:S(2)}) async-start(s8[12582912]{0:T(1024)(128)(4,1)} %bitcast.131), calls=%async_computation.13 | async-start | bytes 8388608
  458.2 13.1 %slice-start.2 = ((s8[12582912]{0:T(1024)(128)(4,1)}), s8[4194304]{0:T(1024)(128)(4,1)S(1)}, s32[]{:S(2)}) async-start(s8[12582912]{0:T(1024)(128)(4,1)} %bitcast.131), calls=%async_computation.14 | async-start | bytes 8388608
  471.3 7.0 copy-start.20
  478.3 3.9 copy-start.1
  478.3 3.9 copy-start.16
  478.3 4.6 copy-start.21
  478.3 4.8 copy-start.42
  485.3 223.3 %reduce-scatter.5.cloned.1.call-start = ((), (), s32[]{:S(2)}) async-start(), calls=%async_computation.8 | async-start | bytes 7299072 | tf_op jit(solution)/shard_map/reduce_scatter | solution.py:167
  485.6 4.3 copy-start.46
  485.6 4.3 copy-start.49
  506.1 343.7 %reduce-scatter.9.cloned.1.call-start = ((), (), s32[]{:S(2)}) async-start(), calls=%async_computation.10 | async-start | bytes 9732096 | tf_op jit(solution)/shard_map/reduce_scatter | solution.py:167
  507.5 4.9 copy-start.11
  507.5 4.9 copy-start.33
  518.2 473.9 %reduce-scatter.11.cloned.1.call-start = ((), (), s32[]{:S(2)}) async-start(), calls=%async_computation.11 | async-start | bytes 9732096 | tf_op jit(solution)/shard_map/reduce_scatter | solution.py:167
  533.5 5.0 copy-start.69
  533.5 6.9 copy-start.74
  580.8 5.3 copy-start.39
  (30 other events, 62.4 us)
Sparse Core Ops, SparseCore 0:
  10.8 62.9 all-gather.4
  76.6 52.8 all-gather.6
  132.3 62.4 all-gather.8
  197.5 62.3 all-gather.10
  485.5 97.9 reduce-scatter.6
  590.5 118.0 reduce-scatter.4
  715.1 134.7 reduce-scatter.8
  857.3 134.6 reduce-scatter.10
where the time goes:
time: 1010 us; the launch traced here: 999 us
  waiting for transfers between devices  558 us (55%)
  matrix products  228 us (23%)
  blocking collectives  82.5 us (8%)
  other arithmetic  75.1 us (7%)
  local copies, waits for them, and re-layouts  39.3 us (4%)
  between operations  15.9 us (2%)
    reduce_scatter x4, waiting for transfers between devices, body(): lax.psum_scatter(totals, ('dp', 'fsdp'), scatter_dimension=0, tiled=True)  400 us
    unnamed x2, blocking collectives  82.5 us
    all_gather x1, waiting for transfers between devices, body(): lax.all_gather(shards[5], ('dp', 'fsdp'), axis=0, tiled=True)  62.6 us
    all_gather x1, waiting for transfers between devices, body(): lax.all_gather(shards[6], ('dp', 'fsdp'), axis=0, tiled=True)  45.1 us
    sub x1, other arithmetic, run_block(): expos = jnp.exp(scores - peak)  33.8 us
    all_gather x1, waiting for transfers between devices, body(): lax.all_gather(shards[3], ('dp', 'fsdp'), axis=0, tiled=True)  33 us
    dot_general x2, matrix products, run_back(): jnp.einsum('qhd,khd->hqk', attn_g, kept['value_rows'], preferred_element_...  27 us
    dot_general x2, matrix products, run_back(): jnp.dot(down_rounded, down_w.T, preferred_element_type=jnp.float32)  26.1 us
  transfers between devices with their start and end apart: 8, of which 7 were waited for; matrix products, arithmetic and copies ran while one was open for 11% of the time, Pallas kernels for 0%

commit v1 on v0

--- a/solution.py
+++ b/solution.py
@@ -1,6 +1,10 @@
+import functools
+
 import jax
 import jax.numpy as jnp
 from jax import lax
+from jax.experimental import pallas as pl
+from jax.experimental.pallas import tpu as pltpu
 from jax.sharding import PartitionSpec as P
 
 HEAD_DIM = 64
@@ -19,16 +23,294 @@
     return jax.nn.gelu(values, approximate=False)
 
 
-def regather(shards):
-    return (
-        lax.all_gather(shards[0], ("dp", "fsdp"), axis=0, tiled=True),
-        lax.all_gather(shards[1], ("dp", "fsdp"), axis=0, tiled=True),
-        lax.all_gather(shards[2], ("dp", "fsdp"), axis=0, tiled=True),
-        lax.all_gather(shards[3], ("dp", "fsdp"), axis=0, tiled=True),
-        lax.all_gather(shards[4], ("dp", "fsdp"), axis=0, tiled=True),
-        lax.all_gather(shards[5], ("dp", "fsdp"), axis=0, tiled=True),
-        lax.all_gather(shards[6], ("dp", "fsdp"), axis=0, tiled=True),
-    )
+MESH = pl.DeviceIdType.MESH
+
+
+def places():
+    d, z = lax.axis_index("dp"), lax.axis_index("fsdp")
+    y, x, c = d // 4, lax.rem(d // 2, 2), lax.rem(d, 2)
+    return d, y, x, c, z
+
+
+def greet(peers):
+    barrier = pltpu.get_barrier_semaphore()
+    for peer in peers:
+        pl.semaphore_signal(barrier, inc=1, device_id=peer, device_id_type=MESH)
+    pl.semaphore_wait(barrier, len(peers))
+
+
+def peers_of(d, y, x, c, z):
+    sideways = (y * 4 + (1 - x) * 2 + c, z)
+    upward = ((1 - y) * 4 + x * 2 + c, z)
+    sibling = (y * 4 + x * 2 + 1 - c, z)
+    along = [(d, lax.rem(z + k, 4)) for k in (1, 2, 3)]
+    return sideways, upward, sibling, along
+
+
+class Gather:
+    def __init__(self, shards, wholes, sems):
+        self.shards, self.wholes = shards, wholes
+        self.z_send, self.z_recv, self.p_send, self.p_recv, self.d_send, self.d_recv, self.own = sems
+        self.d, self.y, self.x, self.c, self.z = places()
+        self.sideways, self.upward, self.sibling, self.along = peers_of(self.d, self.y, self.x, self.c, self.z)
+        self.started = []
+
+    def halves(self, a):
+        width = self.shards[a].shape[2]
+        if width == 128:
+            return ((0, 128),)
+        return ((0, width // 2), (width // 2, width // 2))
+
+    def group(self, a, y, x, cols=None):
+        rows = self.shards[a].shape[0]
+        at = (y * 4 + x * 2 + self.c) * 4 * rows
+        whole = self.wholes[a]
+        if cols is None:
+            return whole.at[pl.ds(at, 4 * rows)]
+        return whole.at[pl.ds(at, 4 * rows), :, pl.ds(*cols)]
+
+    def send(self, src, dst, send, recv, peer):
+        copy = pltpu.make_async_remote_copy(
+            src_ref=src, dst_ref=dst, send_sem=send, recv_sem=recv, device_id=peer, device_id_type=MESH
+        )
+        copy.start()
+        self.started.append(copy)
+        return copy
+
+    def begin(self, a):
+        rows = self.shards[a].shape[0]
+        at = (self.d * 4 + self.z) * rows
+        shard, mine = self.shards[a], self.wholes[a].at[pl.ds(at, rows)]
+        own = pltpu.make_async_copy(shard, mine, self.own.at[a])
+        own.start()
+        along = []
+        for k in range(3):
+            along.append(self.send(shard, mine, self.z_send.at[a, k], self.z_recv.at[a, k], self.along[k]))
+        return own, along
+
+    def to_sibling(self, a, g, y, x):
+        block = self.group(a, y, x)
+        return self.send(block, block, self.d_send.at[a, g], self.d_recv.at[a, g], self.sibling)
+
+    def first(self, a, begun):
+        own, along = begun
+        own.wait()
+        for copy in along:
+            copy.wait_recv()
+        sent = []
+        for h, cols in enumerate(self.halves(a)):
+            block = self.group(a, self.y, self.x, cols)
+            one, two = (self.sideways, self.upward) if h == 0 else (self.upward, self.sideways)
+            sent.append((
+                self.send(block, block, self.p_send.at[a, h, 0], self.p_recv.at[a, h, 0], one),
+                self.send(block, block, self.p_send.at[a, h, 1], self.p_recv.at[a, h, 1], two),
+            ))
+        shared = [self.to_sibling(a, 0, self.y, self.x)]
+        return sent, shared
+
+    def second(self, a, state):
+        sent, shared = state
+        last = []
+        for h, cols in enumerate(self.halves(a)):
+            sent[h][0].wait_recv()
+            y, x = (self.y, 1 - self.x) if h == 0 else (1 - self.y, self.x)
+            block = self.group(a, y, x, cols)
+            two = self.upward if h == 0 else self.sideways
+            last.append(self.send(block, block, self.p_send.at[a, h, 2], self.p_recv.at[a, h, 2], two))
+        return sent, shared, last
+
+    def third(self, a, state):
+        sent, shared, last = state
+        for copies in sent:
+            copies[1].wait_recv()
+        shared.append(self.to_sibling(a, 1, self.y, 1 - self.x))
+        shared.append(self.to_sibling(a, 2, 1 - self.y, self.x))
+        return shared, last
+
+    def fourth(self, a, state):
+        shared, last = state
+        for copy in last:
+            copy.wait_recv()
+        shared.append(self.to_sibling(a, 3, 1 - self.y, 1 - self.x))
+        return shared
+
+    def finish(self, a, shared):
+        for copy in shared:
+            copy.wait_recv()
+
+    def close(self):
+        for copy in self.started:
+            copy.wait_send()
+
+
+def gather_kernel(*refs):
+    shards, wholes, sems = refs[:5], refs[5:10], refs[10:]
+    g = Gather(shards, wholes, sems)
+    greet([g.sideways, g.upward, g.sibling, *g.along])
+    order = (0, 1, 2, 3, 4)
+    state = {a: g.begin(a) for a in order}
+    steps = (g.first, g.second, g.third, g.fourth)
+    for tick in range(len(order) + len(steps) - 1):
+        for late, step in enumerate(steps):
+            if 0 <= tick - late < len(order):
+                a = order[tick - late]
+                state[a] = step(a, state[a])
+    for a in order:
+        g.finish(a, state[a])
+    g.close()
+
+
+def gather_all(shards):
+    count = len(shards)
+    dma = pltpu.SemaphoreType.DMA
+    return pl.pallas_call(
+        gather_kernel,
+        out_shape=[jax.ShapeDtypeStruct((32 * s.shape[0],) + s.shape[1:], s.dtype) for s in shards],
+        in_specs=[pl.BlockSpec(memory_space=pl.ANY)] * count,
+        out_specs=[pl.BlockSpec(memory_space=pl.ANY)] * count,
+        scratch_shapes=[
+            dma((count, 3)), dma((count, 3)), dma((count, 2, 3)), dma((count, 2, 3)), dma((count, 4)), dma((count, 4)), dma((count,)),
+        ],
+        name="gather",
+        compiler_params=pltpu.CompilerParams(collective_id=0, has_side_effects=True),
+    )(*shards)
+
+
+class Reduce:
+    def __init__(self, parts, r0, r1, r2, r3, outs, sems):
+        self.parts, self.r0, self.r1, self.r2, self.r3, self.outs = parts, r0, r1, r2, r3, outs
+        self.d_send, self.d_recv, self.p_send, self.p_recv, self.z_send, self.z_recv = sems
+        self.d, self.y, self.x, self.c, self.z = places()
+        self.sideways, self.upward, self.sibling, self.along = peers_of(self.d, self.y, self.x, self.c, self.z)
+        self.started = []
+
+    send = Gather.send
+
+    def halves(self, a):
+        width = self.outs[a].shape[2]
+        if width == 128:
+            return ((0, 128),)
+        return ((0, width // 2), (width // 2, width // 2))
+
+    def add(self, count, into, into_at, other, other_at, cols):
+        cols = pl.ds(*cols)
+
+        def one(i, carry):
+            into[into_at + i, :, cols] = (
+                into[into_at + i, :, cols].astype(jnp.float32) + other[other_at + i, :, cols].astype(jnp.float32)
+            ).astype(into.dtype)
+            return carry
+
+        lax.fori_loop(0, count, one, 0)
+
+    def begin(self, a):
+        rows = self.outs[a].shape[0]
+        copies = []
+        for g in range(4):
+            src = self.parts[a].at[pl.ds((g * 2 + 1 - self.c) * 4 * rows, 4 * rows)]
+            dst = self.r0[a].at[pl.ds(g * 4 * rows, 4 * rows)]
+            copies.append(self.send(src, dst, self.d_send.at[a, g], self.d_recv.at[a, g], self.sibling))
+        return copies
+
+    def first(self, a, copies):
+        rows = self.outs[a].shape[0]
+        width = self.outs[a].shape[2]
+        for g in range(4):
+            copies[g].wait_recv()
+            self.add(4 * rows, self.r0[a], g * 4 * rows, self.parts[a], (g * 2 + self.c) * 4 * rows, (0, width))
+        sent = []
+        for h, cols in enumerate(self.halves(a)):
+            pair = []
+            for i in range(2):
+                g = (1 - self.y) * 2 + i if h == 0 else i * 2 + 1 - self.x
+                src = self.r0[a].at[pl.ds(g * 4 * rows, 4 * rows), :, pl.ds(*cols)]
+                dst = self.r1[a].at[pl.ds(i * 4 * rows, 4 * rows), :, pl.ds(*cols)]
+                peer = self.upward if h == 0 else self.sideways
+                pair.append(self.send(src, dst, self.p_send.at[a, h, i], self.p_recv.at[a, h, i], peer))
+            sent.append(pair)
+        return sent
+
+    def second(self, a, sent):
+        rows = self.outs[a].shape[0]
+        onward = []
+        for h, cols in enumerate(self.halves(a)):
+            for i in range(2):
+                sent[h][i].wait_recv()
+                g = self.y * 2 + i if h == 0 else i * 2 + self.x
+                self.add(4 * rows, self.r1[a], i * 4 * rows, self.r0[a], g * 4 * rows, cols)
+            far = 1 - self.x if h == 0 else 1 - self.y
+            peer = self.sideways if h == 0 else self.upward
+            src = self.r1[a].at[pl.ds(far * 4 * rows, 4 * rows), :, pl.ds(*cols)]
+            dst = self.r2[a].at[:, :, pl.ds(*cols)]
+            onward.append(self.send(src, dst, self.p_send.at[a, h, 2], self.p_recv.at[a, h, 2], peer))
+        return onward
+
+    def third(self, a, onward):
+        rows = self.outs[a].shape[0]
+        for h, cols in enumerate(self.halves(a)):
+            onward[h].wait_recv()
+            near = self.x if h == 0 else self.y
+            self.add(4 * rows, self.r2[a], 0, self.r1[a], near * 4 * rows, cols)
+        along = []
+        for k in range(3):
+            to = lax.rem(self.z + k + 1, 4)
+            src = self.r2[a].at[pl.ds(to * rows, rows)]
+            dst = self.r3[a].at[pl.ds(k * rows, rows)]
+            along.append(self.send(src, dst, self.z_send.at[a, k], self.z_recv.at[a, k], self.along[k]))
+        return along
+
+    def finish(self, a, along):
+        rows = self.outs[a].shape[0]
+        for copy in along:
+            copy.wait_recv()
+
+        def one(i, carry):
+            total = self.r2[a][self.z * rows + i].astype(jnp.float32)
+            for k in range(3):
+                total = total + self.r3[a][k * rows + i].astype(jnp.float32)
+            self.outs[a][i] = total
+            return carry
+
+        lax.fori_loop(0, rows, one, 0)
+
+    def close(self):
+        for copy in self.started:
+            copy.wait_send()
+
+
+def reduce_kernel(count, *refs):
+    parts, outs = refs[:count], refs[count : 2 * count]
+    r0, r1, r2, r3 = (refs[(2 + k) * count : (3 + k) * count] for k in range(4))
+    g = Reduce(parts, r0, r1, r2, r3, outs, refs[6 * count :])
+    greet([g.sideways, g.upward, g.sibling, *g.along])
+    order = range(count)
+    state = {a: g.begin(a) for a in order}
+    steps = (g.first, g.second, g.third, g.finish)
+    for tick in range(len(order) + len(steps) - 1):
+        for late, step in enumerate(steps):
+            if 0 <= tick - late < len(order):
+                a = order[tick - late]
+                state[a] = step(a, state[a])
+    g.close()
+
+
+def reduce_all(parts):
+    count = len(parts)
+    dma = pltpu.SemaphoreType.DMA
+    scratch = []
+    for blocks in (16, 8, 4, 3):
+        scratch += [pltpu.VMEM((p.shape[0] // 32 * blocks,) + p.shape[1:], p.dtype) for p in parts]
+    return pl.pallas_call(
+        functools.partial(reduce_kernel, count),
+        out_shape=[jax.ShapeDtypeStruct((p.shape[0] // 32,) + p.shape[1:], jnp.float32) for p in parts],
+        in_specs=[pl.BlockSpec(memory_space=pltpu.VMEM)] * count,
+        out_specs=[pl.BlockSpec(memory_space=pltpu.VMEM)] * count,
+        scratch_shapes=scratch + [
+            dma((count, 4)), dma((count, 4)), dma((count, 2, 3)), dma((count, 2, 3)), dma((count, 3)), dma((count, 3)),
+        ],
+        name="reduce",
+        compiler_params=pltpu.CompilerParams(collective_id=1, has_side_effects=True, vmem_limit_bytes=56 << 20),
+    )(*parts)
 
 
 def run_block(inputs, earlier, allowed, weights):
@@ -133,17 +415,38 @@
     return ((ln1_g, qkv_g, wout_g, ln2_g, up_g, down_g), input_g, earlier_g)
 
 
-def body(tokens, doc_ids, pass_embed, ln1_gain, w_qkv, w_out, ln2_gain, w_up, w_down, cotangent):
-    shards = (pass_embed, ln1_gain, w_qkv, w_out, ln2_gain, w_up, w_down)
-    weights = (
-        lax.all_gather(shards[0], ("dp", "fsdp"), axis=0, tiled=True),
-        lax.all_gather(shards[1], ("dp", "fsdp"), axis=0, tiled=True),
-        lax.all_gather(shards[2], ("dp", "fsdp"), axis=0, tiled=True),
-        lax.all_gather(shards[3], ("dp", "fsdp"), axis=0, tiled=True),
-        lax.all_gather(shards[4], ("dp", "fsdp"), axis=0, tiled=True),
-        lax.all_gather(shards[5], ("dp", "fsdp"), axis=0, tiled=True),
-        lax.all_gather(shards[6], ("dp", "fsdp"), axis=0, tiled=True),
-    )
+AXES = ("dp", "fsdp")
+
+
+def gather_weights(near, shards):
+    if not near:
+        return tuple(lax.all_gather(s, AXES, axis=0, tiled=True) for s in shards)
+    embed, ln1, qkv, out, ln2, up, down = shards
+    rows = embed.shape[0]
+    small = jnp.zeros((1, 8, 128), jnp.bfloat16)
+    small = small.at[0, :3, :rows].set(jnp.stack([embed, ln1, ln2]))
+    cut = lambda w: w.reshape(w.shape[0] // 8, 8, w.shape[1])
+    small, out, qkv, up, down = gather_all([small, cut(out), cut(qkv), cut(up), cut(down)])
+    vectors = small[:, :3, :rows].transpose(1, 0, 2).reshape(3, 32 * rows)
+    join = lambda w: w.reshape(w.shape[0] * 8, w.shape[2])
+    return (vectors[0], vectors[1], join(qkv), join(out), vectors[2], join(up), join(down))
+
+
+def reduce_grads(near, totals):
+    if not near:
+        return lax.psum_scatter(totals, AXES, scatter_dimension=0, tiled=True)
+    embed, ln1, qkv, out, ln2, up, down = totals
+    rows = embed.shape[0] // 32
+    small = jnp.stack([embed, ln1, ln2]).reshape(3, 32, rows).transpose(1, 0, 2)
+    small = jnp.zeros((32, 8, 128), jnp.bfloat16).at[:, :3, :rows].set(small.astype(jnp.bfloat16))
+    cut = lambda w: w.astype(jnp.bfloat16).reshape(w.shape[0] // 8, 8, w.shape[1])
+    down, up, out, qkv, small = reduce_all([cut(down), cut(up), cut(out), cut(qkv), small])
+    join = lambda w: w.reshape(w.shape[0] * 8, w.shape[2])
+    return (small[0, 0, :rows], small[0, 1, :rows], join(qkv), join(out), small[0, 2, :rows], join(up), join(down))
+
+
+def body(near, tokens, doc_ids, pass_embed, ln1_gain, w_qkv, w_out, ln2_gain, w_up, w_down, cotangent):
+    weights = gather_weights(near, (pass_embed, ln1_gain, w_qkv, w_out, ln2_gain, w_up, w_down))
     length = tokens.shape[0]
     places = jnp.arange(length, dtype=jnp.int32)
     allowed = (doc_ids[:, None] == doc_ids[None, :]) & (places[None, :] <= places[:, None])
@@ -151,11 +454,9 @@
     inputs = tokens.astype(jnp.float32)
     first_out, first_kept = run_block(inputs, None, allowed, weights)
     earlier = first_kept["own_kv"]
-    weights = regather(shards)
     second_in = first_out + weights[0].astype(jnp.float32)
     second_out, unused = run_block(second_in, earlier, doubled, weights)
     layer_out = second_out.astype(jnp.bfloat16)
-    weights = regather(shards)
     late_grads, second_in_g, earlier_g = run_back(
         second_in, earlier, doubled, weights, cotangent.astype(jnp.float32), None
     )
@@ -164,21 +465,11 @@
         inputs, None, allowed, weights, second_in_g, earlier_g
     )
     totals = (embed_g,) + tuple((a + b for a, b in zip(late_grads, early_grads)))
-    summed = lax.psum_scatter(totals, ("dp", "fsdp"), scatter_dimension=0, tiled=True)
-    return (
-        layer_out,
-        tokens_grad,
-        summed[0],
-        summed[1],
-        summed[2],
-        summed[3],
-        summed[4],
-        summed[5],
-        summed[6],
-    )
+    return (layer_out, tokens_grad, *reduce_grads(near, totals))
 
 
 def solution(mesh):
+    near = dict(mesh.shape) == {"dp": 8, "fsdp": 4}
     placed = (
         P(("dp", "fsdp"), None),
         P(("dp", "fsdp")),
@@ -192,7 +483,7 @@
         P(("dp", "fsdp"), None),
     )
     return jax.shard_map(
-        body,
+        functools.partial(body, near),
         mesh=mesh,
         in_specs=placed,
         out_specs=(

time: 1010 us -> 512 us (0.51)
  waiting for transfers between devices: 558 us -> 0 us
  Pallas kernels: 0 us -> 177 us
  blocking collectives: 82.5 us -> 0 us
  between operations: 15.9 us -> 2.04 us
    reduce_scatter x4 -> x0, waiting for transfers between devices: 400 us -> none  [body(): lax.psum_scatter(totals, ('dp', 'fsdp'), scatter_dimension=0, tiled=True)]
    pallas_call x0 -> x2, Pallas kernels: none -> 177 us  [the longest x1 94.3 us: reduce_all(): pl.pallas_call(functools.partial(reduce_kernel, count), out_shape=[jax.Sh...]
    all_gather x4 -> x0, waiting for transfers between devices: 155 us -> none  [the longest x1 62.6 us: body(): lax.all_gather(shards[5], ('dp', 'fsdp'), axis=0, tiled=True)]
    unnamed x2 -> x0, blocking collectives: 82.5 us -> none
    dot_general x2, matrix products: 25.5 us -> 40.1 us  [run_block(): hidden = jnp.dot(second, up_w, preferred_element_type=jnp.float32)]
    unnamed x181 -> x182, local copies, waits for them, and re-layouts: 24.3 us -> 17.5 us
  transfers between devices with their start and end apart: 8 -> 0, of which waited for: 7 -> 0; matrix products, arithmetic and copies ran while one was open for 11% -> 0% of each run, Pallas kernels for 0% -> 0%
where the time goes in v1:
time: 512 us; the launch traced here: 509 us
  matrix products  219 us (43%)
  Pallas kernels  177 us (35%)
  other arithmetic  73 us (14%)
  local copies, waits for them, and re-layouts  37.7 us (7%)
    pallas_call x1, Pallas kernels, reduce_all(): pl.pallas_call(functools.partial(reduce_kernel, count), out_shape=[jax.Sh...  94.3 us
    pallas_call x1, Pallas kernels, gather_all(): pl.pallas_call(gather_kernel, out_shape=[jax.ShapeDtypeStruct((32 * s.sha...  82.7 us
    dot_general x2, matrix products, run_block(): hidden = jnp.dot(second, up_w, preferred_element_type=jnp.float32)  40.1 us
    sub x1, other arithmetic, run_block(): expos = jnp.exp(scores - peak)  33.3 us
    convert_element_type x2, other arithmetic, run_back(): scores_g = scores_g.astype(jnp.bfloat16)  28.9 us
    dot_general x2, matrix products, run_back(): jnp.einsum('qhd,khd->hqk', attn_g, kept['value_rows'], preferred_element_...  28.9 us
    unnamed x182, local copies, waits for them, and re-layouts  17.5 us
    dot_general x2, matrix products, run_block(): jnp.einsum('hqk,khd->qhd', probs.astype(jnp.bfloat16), value_rows, prefer...  16.9 us

profile of v1, /device:TPU:0, one launch (start us, length us, event | category | flops | bytes accessed | tf_op | source)
XLA Modules:
  0.0 508.6 jit_solution(17000905473904715054)
XLA Ops:
  1.9 82.7 %gather.1 = (bf16[32,8,128]{2,1,0:T(8,128)(2,1)}, bf16[96,8,768]{2,1,0:T(8,128)(2,1)}, bf16[96,8,2304]{2,1,0:T(8,128)(2,1)}, bf16[96,8,3072]{2,1,0:T(8,128)(2,1)}, bf16[384,8,768]{2,1,0:T(8,128)(2,1)}) custom-call(bf16[1,8,128]{2,1,0:T(8,128)(2,1)} %scatter.6.refs_0_, bf16[3,8,768]{2,1,0:T(8,128)(2,1)} %bitcast.244, bf16[3,8,2304]{2,1,0:T(8,128)(2,1)} %bitcast.242, ...), custom_call_target="tpu_custom_call" | custom-call | tf_op jit(solution)/shard_map/gather/pallas_call | solution.py:166
  84.7 0.9 slice_bitcast_fusion.17
  85.8 1.3 convert_reduce_fusion
  87.1 1.5 fusion.77
  89.8 5.8 %convolution_convert_fusion.1 = bf16[512,2304]{1,0:T(8,128)(2,1)} fusion(bf16[96,8,2304]{2,1,0:T(8,128)(2,1)} %get-tuple-element.44, bf16[512,768]{1,0:T(8,128)(2,1)} %param.14, f32[768]{0:T(1024)S(1)} %reshape.427, f32[512]{0:T(512)S(1)} %fusion.112, f32[512]{0:T(512)S(1)} %broadcast_multiply_fusion.3), kind=kOutput, calls=%fused_computation.90 | convolution fusion | flops 1815085056 | bytes 6691840 | tf_op jit(solution)/shard_map/dot_general | solution.py:322
  95.6 3.0 copy.33
  98.8 7.5 %fusion.136 = (f32[12,512]{1,0:T(8,128)S(1)}, f32[12,512,512]{1,2,0:T(8,128)}) fusion(pred[512,512]{0,1:T(8,128)(4,1)S(1)} %fusion.100, bf16[512,3,12,64]{0,3,2,1:T(8,128)(2,1)S(1)} %bitcast.217), kind=kOutput, calls=%fused_computation.228 | convolution fusion | flops 415236608 | bytes 14442496 | tf_op jit(solution)/shard_map/sub | solution.py:335
  106.3 5.9 %fusion.88 = bf16[12,64,512]{2,1,0:T(8,128)(2,1)S(1)} fusion(bf16[512,3,12,64]{0,3,2,1:T(8,128)(2,1)S(1)} %bitcast.218, f32[12,512,512]{1,2,0:T(8,128)} %get-tuple-element.84, f32[12,512]{1,0:T(8,128)S(1)} %get-tuple-element.83), kind=kOutput, calls=%fused_computation.155 | convolution fusion | flops 409337856 | bytes 14188544 | tf_op jit(solution)/shard_map/hqk,khd->qhd/dot_general | solution.py:337
  112.3 0.9 fusion.137
  114.3 19.6 %multiply_convert_fusion.3 = (bf16[512,3072]{1,0:T(8,128)(2,1)}, f32[512,3072]{1,0:T(8,128)}, f32[512,3072]{1,0:T(8,128)}) fusion(bf16[96,8,3072]{2,1,0:T(8,128)(2,1)} %get-tuple-element.46, f32[512,768]{1,0:T(8,128)S(1)} %get-tuple-element.86, f32[768]{0:T(1024)S(1)} %reshape.428, f32[512]{0:T(512)S(1)} %fusion.113, f32[512]{0:T(512)S(1)} %broadcast_multiply_fusion.2), kind=kOutput, calls=%fused_computation.50 | convolution fusion | flops 2519728128 | bytes 22027264 | tf_op jit(solution)/shard_map/dot_general | solution.py:343
  134.1 6.1 %fusion.138 = (f32[512]{0:T(512)S(1)}, f32[512,768]{1,0:T(8,128)S(1)}) fusion(f32[768]{0:T(1024)S(1)} %reshape.429, f32[512,768]{1,0:T(8,128)S(1)} %get-tuple-element.86, bf16[512,3072]{1,0:T(8,128)(2,1)} %get-tuple-element.74, bf16[384,8,768]{2,1,0:T(8,128)(2,1)} %get-tuple-element.47), kind=kOutput, calls=%fused_computation.230 | convolution fusion | flops 2417098240 | bytes 11015168 | tf_op jit(solution)/shard_map/dot_general | solution.py:345
  140.6 3.5 convolution_convert_fusion
  144.1 4.3 copy.35
  148.4 3.1 slice_bitcast_fusion.2
  151.6 10.1 %fusion.101 = f32[12,512,1024]{2,1,0:T(8,128)} fusion(bf16[512,12,64]{0,2,1:T(8,128)(2,1)S(1)} %get-tuple-element.78, bf16[512,12,64]{0,2,1:T(8,128)(2,1)S(1)} %get-tuple-element.105, bf16[512,3,12,64]{0,3,2,1:T(8,128)(2,1)S(1)} %bitcast.216), kind=kOutput, calls=%fused_computation.164 | convolution fusion | flops 808452096 | bytes 27525120 | tf_op jit(solution)/shard_map/qhd,khd->hqk/dot_general | solution.py:331
  161.8 0.9 copy.36
  162.7 33.3 %fusion.139 = (f32[12,512]{1,0:T(8,128)S(1)}, f32[12,512,1024]{2,1,0:T(8,128)}) fusion(f32[12,512,1024]{2,1,0:T(8,128)} %fusion.101, pred[512,1024]{1,0:T(8,128)(4,1)S(1)} %copy.36), kind=kOutput, calls=%fused_computation.231 | output fusion | flops 37749760 | bytes 50880512 | tf_op jit(solution)/shard_map/sub | solution.py:335
  196.0 11.0 %fusion.91 = bf16[12,64,512]{2,1,0:T(8,128)(2,1)S(1)} fusion(bf16[512,12,64]{0,2,1:T(8,128)(2,1)S(1)} %get-tuple-element.79, bf16[512,12,64]{0,2,1:T(8,128)(2,1)} %get-tuple-element.104, f32[12,512,1024]{2,1,0:T(8,128)} %get-tuple-element.91, f32[12,512]{1,0:T(8,128)S(1)} %get-tuple-element.90), kind=kOutput, calls=%fused_computation.156 | convolution fusion | flops 821428224 | bytes 27549696 | tf_op jit(solution)/shard_map/hqk,khd->qhd/dot_general | solution.py:337
  207.0 0.9 fusion.140
  208.3 20.5 %multiply_convert_fusion.2 = (bf16[512,3072]{1,0:T(8,128)(2,1)}, f32[512,3072]{1,0:T(8,128)}, f32[512,3072]{1,0:T(8,128)}) fusion(bf16[96,8,3072]{2,1,0:T(8,128)(2,1)} %get-tuple-element.46, f32[512,768]{1,0:T(8,128)S(1)} %get-tuple-element.93, f32[512]{0:T(512)S(1)} %fusion.115, f32[512]{0:T(512)S(1)} %broadcast_multiply_fusion, f32[768]{0:T(1024)S(1)} %reshape.428), kind=kOutput, calls=%fused_computation.33 | convolution fusion | flops 2519728128 | bytes 22027264 | tf_op jit(solution)/shard_map/dot_general | solution.py:343
  228.9 7.3 %fusion.14 = bf16[512,3072]{1,0:T(8,128)(2,1)S(1)} fusion(f32[512,3072]{1,0:T(8,128)} %get-tuple-element.73, f32[512,3072]{1,0:T(8,128)} %get-tuple-element.94, bf16[512,768]{1,0:T(8,128)(2,1)S(1)} %copy-done.24, bf16[384,8,768]{2,1,0:T(8,128)(2,1)S(1)} %bitcast.249), kind=kOutput, calls=%fused_computation.30 | convolution fusion | flops 2437939200 | bytes 21233664 | tf_op jit(solution)/shard_map/dot_general | solution.py:370
  236.2 3.4 multiply_reduce_fusion.3
  240.5 0.9 copy-done.27
  241.4 1.7 convolution_convert_fusion.3
  243.1 2.3 copy.38
  245.4 16.9 %multiply_reduce_fusion = (f32[12,512]{1,0:T(8,128)S(1)}, f32[12,512,1024]{2,1,0:T(8,128)}) fusion(f32[12,512,1024]{2,1,0:T(8,128)} %get-tuple-element.91, f32[12,512]{1,0:T(8,128)S(1)} %get-tuple-element.90, bf16[512,12,64]{0,2,1:T(8,128)(2,1)} %bitcast.231, bf16[512,12,64]{0,2,1:T(8,128)(2,1)} %copy-done.36, bf16[512,12,64]{0,2,1:T(8,128)(2,1)} %get-tuple-element.104), kind=kOutput, calls=%fused_computation.3 | convolution fusion | flops 827320320 | bytes 52740096 | tf_op jit(solution)/shard_map/qhd,khd->hqk/dot_general | solution.py:386
  262.4 21.8 %multiply_convert_fusion = bf16[12,512,1024]{2,1,0:T(8,128)(2,1)} fusion(f32[12,512,1024]{2,1,0:T(8,128)} %get-tuple-element.97, f32[12,512]{1,0:T(8,128)S(1)} %get-tuple-element.96, f32[12,512,1024]{2,1,0:T(8,128)} %get-tuple-element.91, f32[12,512]{1,0:T(8,128)S(1)} %get-tuple-element.90), kind=kLoop, calls=%fused_computation.2 | loop fusion | flops 25165824 | bytes 62963712 | tf_op jit(solution)/shard_map/convert_element_type | solution.py:390
  284.2 8.5 %multiply_bitcast_fusion.2 = bf16[512,1,12,64]{0,3,2,1:T(8,128)(2,1)S(1)} fusion(bf16[12,512,1024]{2,1,0:T(8,128)(2,1)} %multiply_convert_fusion, bf16[512,12,64]{0,2,1:T(8,128)(2,1)S(1)} %copy-done.12, bf16[512,12,64]{0,2,1:T(8,128)(2,1)S(1)} %copy-done.14), kind=kOutput, calls=%fused_computation.140 | convolution fusion | flops 809238528 | bytes 14942208 | tf_op jit(solution)/shard_map/hqk,khd->qhd/dot_general | solution.py:392
  292.7 7.2 %multiply_bitcast_fusion = f32[1024,12,64]{0,2,1:T(8,128)S(1)} fusion(bf16[12,512,1024]{2,1,0:T(8,128)(2,1)} %multiply_convert_fusion, bf16[512,3,12,64]{0,3,2,1:T(8,128)(2,1)} %bitcast.215), kind=kOutput, calls=%fused_computation.97 | convolution fusion | flops 806092800 | bytes 16515072 | tf_op jit(solution)/shard_map/hqk,qhd->khd/dot_general | solution.py:396
  299.9 1.7 copy-done.5
  301.7 9.9 %fusion.70 = f32[1024,12,64]{0,2,1:T(8,128)S(1)} fusion(bf16[512,12,64]{0,2,1:T(8,128)(2,1)S(1)} %bitcast.232, f32[12,512,1024]{2,1,0:T(8,128)} %get-tuple-element.91, f32[12,512]{1,0:T(8,128)S(1)} %get-tuple-element.90), kind=kOutput, calls=%fused_computation.116 | convolution fusion | flops 817889280 | bytes 29122560 | tf_op jit(solution)/shard_map/hqk,qhd->khd/dot_general | solution.py:383
  312.1 1.3 copy-done.45
  313.4 2.3 copy-done.74
  315.7 2.4 multiply_reduce_fusion.4
  319.8 8.9 %add_convert_fusion.3 = bf16[512,3072]{1,0:T(8,128)(2,1)} fusion(f32[512,3072]{1,0:T(8,128)} %get-tuple-element.75, f32[512,3072]{1,0:T(8,128)} %get-tuple-element.87, bf16[384,8,768]{2,1,0:T(8,128)(2,1)S(1)} %bitcast.251, f32[512,768]{1,0:T(8,128)S(1)} %get-tuple-element.65), kind=kOutput, calls=%fused_computation.32 | convolution fusion | flops 2438332416 | bytes 22020096 | tf_op jit(solution)/shard_map/dot_general | solution.py:370
  328.7 6.2 %multiply_reduce_fusion.2 = (f32[768]{0:T(1024)S(1)}, f32[512]{0:T(512)S(1)}, f32[512,768]{1,0:T(8,128)S(1)}) fusion(f32[512,768]{1,0:T(8,128)S(1)} %copy-done.16, f32[512]{0:T(512)S(1)} %copy-done.71, f32[512]{0:T(512)S(1)} %copy-done.62, f32[768]{0:T(1024)S(1)} %reshape.428, bf16[512,3072]{1,0:T(8,128)(2,1)} %add_convert_fusion.3, ...), kind=kOutput, calls=%fused_computation.131 | convolution fusion | flops 2418670336 | bytes 11022336 | tf_op jit(solution)/shard_map/dot_general | solution.py:374
  335.8 1.0 copy-done.35
  336.8 1.7 convolution_convert_fusion.2
  338.5 2.3 copy.39
  340.8 12.0 %multiply_reduce_fusion.1 = (f32[12,512]{1,0:T(8,128)S(1)}, f32[12,512,512]{1,2,0:T(8,128)}) fusion(f32[12,512,512]{1,2,0:T(8,128)} %get-tuple-element.84, f32[12,512]{1,0:T(8,128)S(1)} %copy-done.58, bf16[512,12,64]{0,2,1:T(8,128)(2,1)} %bitcast.233, bf16[512,3,12,64]{0,3,2,1:T(8,128)(2,1)} %bitcast.220), kind=kOutput, calls=%fused_computation.8 | convolution fusion | flops 412084224 | bytes 26787840 | tf_op jit(solution)/shard_map/qhd,khd->hqk/dot_general | solution.py:386
  352.8 7.1 %multiply_convert_fusion.1 = bf16[12,512,512]{1,2,0:T(8,128)(2,1)S(1)} fusion(f32[12,512,512]{1,2,0:T(8,128)} %get-tuple-element.101, f32[12,512]{1,0:T(8,128)S(1)} %get-tuple-element.100, f32[12,512,512]{1,2,0:T(8,128)S(1)} %bitcast.224, f32[12,512]{1,0:T(8,128)S(1)} %copy-done.58), kind=kLoop, calls=%fused_computation.7 | loop fusion | flops 12582912 | bytes 31506432 | tf_op jit(solution)/shard_map/convert_element_type | solution.py:390
  360.0 1.1 multiply_bitcast_fusion.1
  361.1 0.7 copy-done.6
  361.9 2.0 fusion.80
  363.9 3.7 fusion.79
  367.9 0.8 copy-done.8
  368.8 2.0 copy-done.75
  370.8 2.2 fusion.78
  373.1 0.8 fusion.76
  375.2 4.1 fusion.128
  379.3 4.3 fusion.49.refs_3_
  383.6 0.8 fusion.142
  384.8 2.0 fusion.87.refs_2_
  386.8 0.7 copy-done.30
  387.5 2.8 fusion.129
  390.4 4.7 fusion.50.refs_1_
  395.1 2.7 fusion.141
  397.8 4.4 fusion.69.refs_0_
  402.2 94.3 %reduce.17 = (f32[12,8,768]{2,1,0:T(8,128)}, f32[3,8,3072]{2,1,0:T(8,128)}, f32[3,8,768]{2,1,0:T(8,128)}, f32[3,8,2304]{2,1,0:T(8,128)}, f32[1,8,128]{2,1,0:T(8,128)}) custom-call(bf16[384,8,768]{2,1,0:T(8,128)(2,1)} %fusion.69.refs_0_, bf16[96,8,3072]{2,1,0:T(8,128)(2,1)} %fusion.50.refs_1_, bf16[96,8,768]{2,1,0:T(8,128)(2,1)} %fusion.87.refs_2_, ...), custom_call_target="tpu_custom_call" | custom-call | tf_op jit(solution)/shard_map/reduce/pallas_call | solution.py:303
  496.5 1.4 slice_bitcast_fusion.18
  497.9 1.7 add_add_fusion.4
  499.6 5.9 %add_convert_fusion.5 = bf16[512,768]{1,0:T(8,128)(2,1)} fusion(f32[512,768]{1,0:T(8,128)S(1)} %copy-done.1, bf16[512,3072]{1,0:T(8,128)(2,1)S(1)} %copy-done.77, bf16[384,8,768]{2,1,0:T(8,128)(2,1)} %get-tuple-element.47), kind=kOutput, calls=%fused_computation.143 | convolution fusion | flops 2416705536 | bytes 10223616 | tf_op jit(solution)/shard_map/dot_general | solution.py:345
  506.9 0.7 copy.57
  507.6 0.7 copy.58
  (219 shorter events, 12.2 us)
Async XLA Ops:
  85.7 54.8 %copy-start.42 = (f32[768]{0:T(1024)}, f32[768]{0:T(1024)S(1)}, u32[]{:S(2)}) copy-start(f32[768]{0:T(1024)S(1)} %reshape.427) | copy-start | bytes 9220
  95.6 3.0 copy-start.69
  98.6 7.7 %copy-start.3 = (bf16[512,2304]{0,1:T(8,128)(2,1)}, bf16[512,2304]{0,1:T(8,128)(2,1)S(1)}, u32[]{:S(2)}) copy-start(bf16[512,2304]{0,1:T(8,128)(2,1)S(1)} %copy.33) | copy-start | bytes 7077892
  106.3 6.0 %copy-start.57 = (f32[12,512]{1,0:T(8,128)}, f32[12,512]{1,0:T(8,128)S(1)}, u32[]{:S(2)}) copy-start(f32[12,512]{1,0:T(8,128)S(1)} %get-tuple-element.83) | copy-start | bytes 73732
  106.3 6.0 %copy-start.7 = (bf16[512,768]{1,0:T(8,128)(2,1)S(1)}, bf16[512,768]{1,0:T(8,128)(2,1)}, u32[]{:S(2)}) copy-start(bf16[512,768]{1,0:T(8,128)(2,1)} %param.14) | copy-start | bytes 2359300
  106.3 6.0 %copy-start.33 = (bf16[96,8,768]{2,1,0:T(8,128)(2,1)S(1)}, bf16[96,8,768]{2,1,0:T(8,128)(2,1)}, u32[]{:S(2)}) copy-start(bf16[96,8,768]{2,1,0:T(8,128)(2,1)} %get-tuple-element.45) | copy-start | bytes 3538948
  113.2 20.9 %copy-start.15 = (f32[512,768]{1,0:T(8,128)}, f32[512,768]{1,0:T(8,128)S(1)}, u32[]{:S(2)}) copy-start(f32[512,768]{1,0:T(8,128)S(1)} %get-tuple-element.86) | copy-start | bytes 4718596
  113.2 20.7 %copy-start.61 = (f32[512]{0:T(512)}, f32[512]{0:T(512)S(1)}, u32[]{:S(2)}) copy-start(f32[512]{0:T(512)S(1)} %broadcast_multiply_fusion.2) | copy-start | bytes 6148
  114.2 19.7 %copy-start.70 = (f32[512]{0:T(512)}, f32[512]{0:T(512)S(1)}, u32[]{:S(2)}) copy-start(f32[512]{0:T(512)S(1)} %fusion.113) | copy-start | bytes 6148
  134.1 6.5 %copy-start.73 = (bf16[96,8,2304]{2,1,0:T(8,128)(2,1)S(1)}, bf16[96,8,2304]{2,1,0:T(8,128)(2,1)}, u32[]{:S(2)}) copy-start(bf16[96,8,2304]{2,1,0:T(8,128)(2,1)} %get-tuple-element.44) | copy-start | bytes 10616836
  140.2 3.9 copy-start.49
  140.5 3.6 copy-start.67
  140.6 3.5 copy-start.55
  148.4 3.1 copy-start.2
  151.5 10.1 %copy-start.11 = (bf16[512,12,64]{0,2,1:T(8,128)(2,1)}, bf16[512,12,64]{0,2,1:T(8,128)(2,1)S(1)}, u32[]{:S(2)}) copy-start(bf16[512,12,64]{0,2,1:T(8,128)(2,1)S(1)} %get-tuple-element.78) | copy-start | bytes 2359300
  151.6 10.1 %copy-start.13 = (bf16[512,12,64]{0,2,1:T(8,128)(2,1)}, bf16[512,12,64]{0,2,1:T(8,128)(2,1)S(1)}, u32[]{:S(2)}) copy-start(bf16[512,12,64]{0,2,1:T(8,128)(2,1)S(1)} %get-tuple-element.105) | copy-start | bytes 2359300
  151.6 44.5 %copy-start.36 = (bf16[512,12,64]{0,2,1:T(8,128)(2,1)}, bf16[512,12,64]{0,2,1:T(8,128)(2,1)S(1)}, u32[]{:S(2)}) copy-start(bf16[512,12,64]{0,2,1:T(8,128)(2,1)S(1)} %get-tuple-element.79) | copy-start | bytes 2359300
  196.0 11.0 %copy-start.34 = (bf16[96,8,768]{2,1,0:T(8,128)(2,1)S(1)}, bf16[96,8,768]{2,1,0:T(8,128)(2,1)}, u32[]{:S(2)}) copy-start(bf16[96,8,768]{2,1,0:T(8,128)(2,1)} %get-tuple-element.45) | copy-start | bytes 3538948
  207.0 21.8 %slice-start.3 = ((s8[4718592]{0:T(1024)(128)(4,1)}), s8[4194304]{0:T(1024)(128)(4,1)S(1)}, s32[]{:S(2)}) async-start(s8[4718592]{0:T(1024)(128)(4,1)} %bitcast.248), calls=%async_computation.3 | async-start | bytes 8388608
  207.0 29.1 %slice-start.7 = ((s8[4718592]{0:T(1024)(128)(4,1)}), s8[4194304]{0:T(1024)(128)(4,1)S(1)}, s32[]{:S(2)}) async-start(s8[4718592]{0:T(1024)(128)(4,1)} %bitcast.252), calls=%async_computation.7 | async-start | bytes 8388608
  207.9 31.7 %copy-start = (f32[512,768]{1,0:T(8,128)}, f32[512,768]{1,0:T(8,128)S(1)}, u32[]{:S(2)}) copy-start(f32[512,768]{1,0:T(8,128)S(1)} %get-tuple-element.93) | copy-start | bytes 4718596
  207.9 31.6 %copy-start.46 = (f32[512]{0:T(512)}, f32[512]{0:T(512)S(1)}, u32[]{:S(2)}) copy-start(f32[512]{0:T(512)S(1)} %broadcast_multiply_fusion) | copy-start | bytes 6148
  208.3 31.3 %copy-start.51 = (f32[512]{0:T(512)}, f32[512]{0:T(512)S(1)}, u32[]{:S(2)}) copy-start(f32[512]{0:T(512)S(1)} %fusion.115) | copy-start | bytes 6148
  208.3 20.6 %copy-start.24 = (bf16[512,768]{1,0:T(8,128)(2,1)S(1)}, bf16[512,768]{1,0:T(8,128)(2,1)}, u32[]{:S(2)}) copy-start(bf16[512,768]{1,0:T(8,128)(2,1)} %param.23) | copy-start | bytes 2359300
  208.3 20.5 %slice-start.4 = ((s8[4718592]{0:T(1024)(128)(4,1)}), s8[524288]{0:T(1024)(128)(4,1)S(1)}, s32[]{:S(2)}) async-start(s8[4718592]{0:T(1024)(128)(4,1)} %bitcast.248), calls=%async_computation.4 | async-start | bytes 1048576
  208.3 27.9 %slice-start.8 = ((s8[4718592]{0:T(1024)(128)(4,1)}), s8[524288]{0:T(1024)(128)(4,1)S(1)}, s32[]{:S(2)}) async-start(s8[4718592]{0:T(1024)(128)(4,1)} %bitcast.252), calls=%async_computation.8 | async-start | bytes 1048576
  236.2 3.4 copy-start.29
  262.4 21.8 %copy-start.12 = (bf16[512,12,64]{0,2,1:T(8,128)(2,1)S(1)}, bf16[512,12,64]{0,2,1:T(8,128)(2,1)}, u32[]{:S(2)}) copy-start(bf16[512,12,64]{0,2,1:T(8,128)(2,1)} %copy-done.11) | copy-start | bytes 2359300
  262.4 21.8 %copy-start.14 = (bf16[512,12,64]{0,2,1:T(8,128)(2,1)S(1)}, bf16[512,12,64]{0,2,1:T(8,128)(2,1)}, u32[]{:S(2)}) copy-start(bf16[512,12,64]{0,2,1:T(8,128)(2,1)} %copy-done.13) | copy-start | bytes 2359300
  292.7 9.0 %copy-start.37 = (bf16[512,768]{0,1:T(8,128)(2,1)S(1)}, bf16[512,768]{0,1:T(8,128)(2,1)}, u32[]{:S(2)}) copy-start(bf16[512,768]{0,1:T(8,128)(2,1)} %copy.38) | copy-start | bytes 2359300
  311.7 4.0 copy-start.74
  311.8 7.9 %slice-start.5 = ((s8[4718592]{0:T(1024)(128)(4,1)}), s8[524288]{0:T(1024)(128)(4,1)S(1)}, s32[]{:S(2)}) async-start(s8[4718592]{0:T(1024)(128)(4,1)} %bitcast.250), calls=%async_computation.5 | async-start | bytes 1048576
  313.4 4.8 copy-start.10
  315.7 4.0 slice-start.6
  319.7 15.8 %copy-start.20 = (f32[512,768]{1,0:T(8,128)}, f32[512,768]{1,0:T(8,128)S(1)}, u32[]{:S(2)}) copy-start(f32[512,768]{1,0:T(8,128)S(1)} %get-tuple-element.65) | copy-start | bytes 4718596
  319.7 8.9 %copy-start.16 = (f32[512,768]{1,0:T(8,128)S(1)}, f32[512,768]{1,0:T(8,128)}, u32[]{:S(2)}) copy-start(f32[512,768]{1,0:T(8,128)} %copy-done.15) | copy-start | bytes 4718596
  319.7 8.9 %copy-start.62 = (f32[512]{0:T(512)S(1)}, f32[512]{0:T(512)}, u32[]{:S(2)}) copy-start(f32[512]{0:T(512)} %copy-done.61) | copy-start | bytes 6148
  319.8 8.9 %copy-start.71 = (f32[512]{0:T(512)S(1)}, f32[512]{0:T(512)}, u32[]{:S(2)}) copy-start(f32[512]{0:T(512)} %copy-done.70) | copy-start | bytes 6148
  328.7 6.2 %copy-start.66 = (f32[512]{0:T(512)S(1)}, f32[512]{0:T(512)}, u32[]{:S(2)}) copy-start(f32[512]{0:T(512)} %copy-done.65) | copy-start | bytes 6148
  336.8 4.0 copy-start.58
  340.8 12.0 %slice-start = ((s8[12582912]{0:T(1024)(128)(4,1)}), s8[4194304]{0:T(1024)(128)(4,1)S(1)}, s32[]{:S(2)}) async-start(s8[12582912]{0:T(1024)(128)(4,1)} %bitcast.223), calls=%async_computation | async-start | bytes 8388608
  340.8 12.0 %slice-start.1 = ((s8[12582912]{0:T(1024)(128)(4,1)}), s8[4194304]{0:T(1024)(128)(4,1)S(1)}, s32[]{:S(2)}) async-start(s8[12582912]{0:T(1024)(128)(4,1)} %bitcast.223), calls=%async_computation.1 | async-start | bytes 8388608
  340.8 12.0 %slice-start.2 = ((s8[12582912]{0:T(1024)(128)(4,1)}), s8[4194304]{0:T(1024)(128)(4,1)S(1)}, s32[]{:S(2)}) async-start(s8[12582912]{0:T(1024)(128)(4,1)} %bitcast.223), calls=%async_computation.2 | async-start | bytes 8388608
  352.8 7.1 %copy-start.4 = (bf16[512,2304]{0,1:T(8,128)(2,1)S(1)}, bf16[512,2304]{0,1:T(8,128)(2,1)}, u32[]{:S(2)}) copy-start(bf16[512,2304]{0,1:T(8,128)(2,1)} %copy-done.3) | copy-start | bytes 7077892
  367.7 3.1 copy-start.75
  367.9 5.1 copy-start.31
  370.7 3.5 copy-start.72
  375.2 4.1 copy-start.9
  375.2 4.1 copy-start.32
  379.3 4.3 copy-start.23
  379.3 4.3 copy-start.28
  384.7 2.8 copy-start.30
  384.7 2.8 copy-start.47
  384.8 2.8 copy-start.52
  387.5 2.8 copy-start.17
  387.5 2.8 copy-start.79
  390.4 4.8 copy-start.26
  390.4 4.7 copy-start.76
  402.2 95.7 %copy-start.19 = (f32[512,768]{1,0:T(8,128)S(1)}, f32[512,768]{1,0:T(8,128)}, u32[]{:S(2)}) copy-start(f32[512,768]{1,0:T(8,128)} %copy-done.18) | copy-start | bytes 4718596
  496.5 3.1 copy-start.77
  499.6 5.9 %copy-start.44 = (f32[3,8,2304]{2,1,0:T(8,128)S(1)}, f32[3,8,2304]{2,1,0:T(8,128)}, u32[]{:S(2)}) copy-start(f32[3,8,2304]{2,1,0:T(8,128)} %get-tuple-element.49) | copy-start | bytes 663556
  499.6 6.6 %copy-start.48 = (f32[3,8,768]{2,1,0:T(8,128)S(1)}, f32[3,8,768]{2,1,0:T(8,128)}, u32[]{:S(2)}) copy-start(f32[3,8,768]{2,1,0:T(8,128)} %get-tuple-element.50) | copy-start | bytes 221188
  499.6 7.3 %copy-start.41 = (f32[3,8,3072]{2,1,0:T(8,128)S(1)}, f32[3,8,3072]{2,1,0:T(8,128)}, u32[]{:S(2)}) copy-start(f32[3,8,3072]{2,1,0:T(8,128)} %get-tuple-element.51) | copy-start | bytes 884740
  499.6 8.0 %copy-start.40 = (f32[12,8,768]{2,1,0:T(8,128)S(1)}, f32[12,8,768]{2,1,0:T(8,128)}, u32[]{:S(2)}) copy-start(f32[12,8,768]{2,1,0:T(8,128)} %get-tuple-element.52) | copy-start | bytes 884740
  (25 other events, 38.9 us)

commit v2 on v1

--- a/solution.py
+++ b/solution.py
@@ -1,4 +1,5 @@
 import functools
+import math
 
 import jax
 import jax.numpy as jnp
@@ -8,19 +9,6 @@
 from jax.sharding import PartitionSpec as P
 
 HEAD_DIM = 64
-
-
-EPS = 1e-05
-
-
-def layer_norm(values, gain):
-    center = values - jnp.mean(values, -1, keepdims=True)
-    spread = jnp.mean(center * center, -1, keepdims=True)
-    return center * lax.rsqrt(spread + EPS) * gain
-
-
-def exact_gelu(values):
-    return jax.nn.gelu(values, approximate=False)
 
 
 MESH = pl.DeviceIdType.MESH
@@ -313,159 +301,531 @@
     )(*parts)
 
 
-def run_block(inputs, earlier, allowed, weights):
-    embed, ln1_w, qkv_w, out_w, ln2_w, up_w, down_w = weights
-    length, model_width = inputs.shape
-    head_count = model_width // HEAD_DIM
-    scale = HEAD_DIM ** (-0.5)
-    normed = layer_norm(inputs, ln1_w.astype(jnp.float32)).astype(jnp.bfloat16)
-    qkv = jnp.dot(normed, qkv_w, preferred_element_type=jnp.float32).astype(jnp.bfloat16)
-    qkv = qkv.reshape(length, 3, head_count, HEAD_DIM)
-    queries, own_keys, own_values = (qkv[:, 0], qkv[:, 1], qkv[:, 2])
-    if earlier is None:
-        key_rows, value_rows = (own_keys, own_values)
-    else:
-        key_rows = jnp.concatenate([earlier[0], own_keys], 0)
-        value_rows = jnp.concatenate([earlier[1], own_values], 0)
-    scores = (
-        jnp.einsum("qhd,khd->hqk", queries, key_rows, preferred_element_type=jnp.float32) * scale
+EPS = 1e-05
+QB = 256
+SCALE = HEAD_DIM ** (-0.5)
+NT = (((1,), (1,)), ((), ()))
+
+
+def dot(left, right):
+    return jnp.dot(left, right, preferred_element_type=jnp.float32)
+
+
+def dot_nt(left, right):
+    return lax.dot_general(left, right, NT, preferred_element_type=jnp.float32)
+
+
+def tiles(count, step):
+    def one(i, carry):
+        step(i)
+        return carry
+
+    lax.fori_loop(0, count, one, 0)
+
+
+def at(i, size):
+    return pl.ds(pl.multiple_of(i * size, size), size)
+
+
+def weight_columns(w, i, size):
+    block = w[:, :, at(i, size)]
+    return block.reshape(block.shape[0] * 8, size)
+
+
+def weight_rows(w, i, size):
+    block = w[pl.ds(i * (size // 8), size // 8)]
+    return block.reshape(size, block.shape[2])
+
+
+def normal(u):
+    center = u - jnp.mean(u, -1, keepdims=True)
+    spread = lax.rsqrt(jnp.mean(center * center, -1, keepdims=True) + EPS)
+    return center * spread, spread
+
+
+def norm_rows(u_ref, gain, out_ref):
+    def step(i):
+        hat, spread = normal(u_ref[at(i, 128)].astype(jnp.float32))
+        out_ref[at(i, 128)] = (hat * gain).astype(jnp.bfloat16)
+
+    tiles(u_ref.shape[0] // 128, step)
+
+
+def gelu_both(x):
+    e = jnp.exp(x * x * -0.5)
+    t = 1.0 / (1.0 + jnp.abs(x) * (0.3275911 * 0.5**0.5))
+    poly = 0.5 * 1.061405429
+    for term in (-1.453152027, 1.421413741, -0.284496736, 0.254829592):
+        poly = poly * t + 0.5 * term
+    tail = poly * t * e
+    cdf = jnp.where(x >= 0, 1.0 - tail, tail)
+    return x * cdf, cdf + x * e * (0.5 / math.pi) ** 0.5
+
+
+def split_heads(block, axis):
+    half = lax.broadcasted_iota(jnp.int32, block.shape, axis) < HEAD_DIM
+    zero = jnp.zeros_like(block)
+    return jnp.where(half, block, zero), jnp.where(half, zero, block)
+
+
+def attend(qkvs, bias_ref, p_refs, rl_ref, o_ref, ot_ref):
+    model = o_ref.shape[1]
+    own = qkvs[-1]
+
+    def step(pair):
+        lanes = at(pair, 128)
+        keys, values = [], []
+        for ref in qkvs:
+            keys.append(ref[:, pl.ds(pl.multiple_of(model + pair * 128, 128), 128)])
+            values.append(ref[:, pl.ds(pl.multiple_of(2 * model + pair * 128, 128), 128)].T)
+        for b in range(own.shape[0] // QB):
+            span = (b + 1) * QB
+            queries = split_heads(own[b * QB : span, lanes] * SCALE, 1)
+            bias = bias_ref[:span, b * QB : span]
+            halves = []
+            for h in range(2):
+                scores = [dot_nt(k[:span], queries[h]) + bias for k in keys]
+                peak = jnp.max(scores[0], 0, keepdims=True)
+                for s in scores[1:]:
+                    peak = jnp.maximum(peak, jnp.max(s, 0, keepdims=True))
+                total, out = None, None
+                for n, s in enumerate(scores):
+                    p = jnp.exp(s - peak)
+                    part = jnp.sum(p, 0, keepdims=True)
+                    p = p.astype(jnp.bfloat16)
+                    p_refs[b][pair, h, n * span : (n + 1) * span] = p
+                    product = dot(values[n][h * HEAD_DIM : (h + 1) * HEAD_DIM, :span], p)
+                    total = part if total is None else total + part
+                    out = product if out is None else out + product
+                scale = 1.0 / total
+                rl_ref[pair, h : h + 1, b * QB : span] = scale
+                halves.append(out * scale)
+            both = jnp.concatenate(halves, 0)
+            ot_ref[at(pair, 128), b * QB : span] = both
+            o_ref[b * QB : span, lanes] = both.astype(jnp.bfloat16).T
+
+    tiles(model // 128, step)
+
+
+def attend_back(qkvs, p_refs, do_ref, ot_ref, dqkv_ref, dkv_refs):
+    model = do_ref.shape[0]
+    own = qkvs[-1]
+
+    def step(pair):
+        lanes = at(pair, 128)
+        rows = at(pair, 128)
+        right = [pl.ds(pl.multiple_of(n * model + pair * 128, 128), 128) for n in range(3)]
+        keys = [ref[:, right[1]] for ref in qkvs]
+        values = [ref[:, right[2]] for ref in qkvs]
+        turned = [k.T for k in keys]
+        dk, dv = [None] * len(qkvs), [None] * len(qkvs)
+        for b in reversed(range(own.shape[0] // QB)):
+            span = (b + 1) * QB
+            block = slice(b * QB, span)
+            queries = split_heads(own[block, lanes] * SCALE, 1)
+            do = do_ref[rows, block]
+            do_down = split_heads(do, 0)
+            do_across = split_heads(do.T, 1)
+            product = do.astype(jnp.float32) * ot_ref[rows, block]
+            dq = []
+            for h in range(2):
+                delta = jnp.sum(product[h * HEAD_DIM : (h + 1) * HEAD_DIM], 0, keepdims=True)
+                dq_head = None
+                for n in range(len(qkvs)):
+                    p = p_refs[b][pair, h, n * span : (n + 1) * span]
+                    ds = dot(values[n][:span], do_down[h]) - delta
+                    ds = (p.astype(jnp.float32) * ds).astype(jnp.bfloat16)
+                    more_dv, more_dk = dot(p, do_across[h]), dot(ds, queries[h])
+                    more_dq = dot(turned[n][h * HEAD_DIM : (h + 1) * HEAD_DIM, :span], ds)
+                    dq_head = more_dq if dq_head is None else dq_head + more_dq
+                    if dk[n] is None:
+                        dk[n], dv[n] = more_dk, more_dv
+                    elif dk[n].shape[0] == span:
+                        dk[n], dv[n] = dk[n] + more_dk, dv[n] + more_dv
+                    else:
+                        dk[n] = jnp.concatenate([dk[n][:span] + more_dk, dk[n][span:]], 0)
+                        dv[n] = jnp.concatenate([dv[n][:span] + more_dv, dv[n][span:]], 0)
+                dq.append(dq_head)
+            dq = (jnp.concatenate(dq, 0) * SCALE).astype(jnp.bfloat16)
+            dqkv_ref[block, lanes] = dq.T
+        for n, ref in enumerate(dkv_refs):
+            if ref is not None and n < len(qkvs) - 1:
+                ref[:, lanes] = dk[n]
+                ref[:, right[1]] = dv[n]
+        extra = dkv_refs[-1]
+        dk, dv = dk[-1], dv[-1]
+        if extra is not None:
+            dk, dv = dk + extra[:, lanes], dv + extra[:, right[1]]
+        dqkv_ref[:, right[1]] = dk.astype(jnp.bfloat16)
+        dqkv_ref[:, right[2]] = dv.astype(jnp.bfloat16)
+
+    tiles(model // 128, step)
+
+
+def project(left_ref, w, add_ref, out_ref, shift=None, size=256):
+    def step(i):
+        value = dot(left_ref[...], weight_columns(w, i, size))
+        if add_ref is not None:
+            value = add_ref[:, at(i, size)].astype(jnp.float32) + value
+        if shift is not None:
+            value = value + shift[:, at(i, size)]
+        out_ref[:, at(i, size)] = value.astype(out_ref.dtype)
+
+    tiles(w.shape[2] // size, step)
+
+
+def project_back(left_ref, w, out_ref, size=256):
+    def step(i):
+        out_ref[:, at(i, size)] = dot_nt(left_ref[...], weight_rows(w, i, size)).astype(out_ref.dtype)
+
+    tiles(w.shape[0] * 8 // size, step)
+
+
+def forward_pass(u_ref, qkv_before, bias_ref, gains, w, keep, out_ref, shift, ready):
+    norm_rows(u_ref, gains[0], keep["a"])
+    turn(keep["a"], keep["at"])
+    ready("qkv")
+    project(keep["a"], w["qkv"], None, keep["qkv"])
+    qkvs = [keep["qkv"]] if qkv_before is None else [qkv_before, keep["qkv"]]
+    attend(qkvs, bias_ref, keep["p"], keep["rl"], keep["o"], keep["ot"])
+    ready("out")
+    project(keep["o"], w["out"], u_ref, keep["m"])
+    norm_rows(keep["m"], gains[1], keep["b"])
+    turn(keep["b"], keep["bt"])
+    ready("up")
+
+    def step(i):
+        hidden = dot(keep["b"][...], weight_columns(w["up"], i, 256))
+        active, slope = gelu_both(hidden)
+        active = active.astype(jnp.bfloat16)
+        keep["f"][:, at(i, 256)] = active
+        keep["ft"][at(i, 256)] = active.T
+        keep["gp"][:, at(i, 256)] = slope.astype(jnp.bfloat16)
+
+    tiles(w["up"].shape[2] // 256, step)
+    ready("down")
+    project(keep["f"], w["down"], keep["m"], out_ref, shift)
+
+
+def norm_back(u_ref, gain, dy_ref, add_ref, out_ref, rounded_ref, gain_grad_ref, sum_ref=None):
+    def step(i, totals):
+        total, whole = totals
+        hat, spread = normal(u_ref[at(i, 128)].astype(jnp.float32))
+        dy = dy_ref[at(i, 128)]
+        total = total + jnp.sum((dy * hat).reshape(16, 8, dy.shape[1]), 0)
+        dy = dy * gain
+        down = dy - jnp.mean(dy, -1, keepdims=True) - hat * jnp.mean(dy * hat, -1, keepdims=True)
+        value = add_ref[at(i, 128)].astype(jnp.float32) + spread * down
+        out_ref[at(i, 128)] = value
+        if rounded_ref is not None:
+            rounded_ref[at(i, 128)] = value.astype(jnp.bfloat16)
+        if sum_ref is not None:
+            whole = whole + jnp.sum(value.reshape(16, 8, dy.shape[1]), 0)
+        return total, whole
+
+    zero = jnp.zeros((8, u_ref.shape[1]), jnp.float32)
+    total, whole = lax.fori_loop(0, u_ref.shape[0] // 128, step, (zero, zero))
+    gain_grad_ref[...] = jnp.broadcast_to(jnp.sum(total, 0, keepdims=True), gain_grad_ref.shape)
+    if sum_ref is not None:
+        sum_ref[...] = jnp.broadcast_to(jnp.sum(whole, 0, keepdims=True), sum_ref.shape)
+
+
+def staged(before, count, piece, stage, sems):
+    def copy(i):
+        slot = lax.rem(i, 2)
+        return pltpu.make_async_copy(piece(before, i), stage.at[slot], sems.at[slot])
+
+    copy(0).start()
+
+    def take(i):
+        @pl.when(i + 1 < count)
+        def _():
+            copy(i + 1).start()
+
+        copy(i).wait()
+        return stage[lax.rem(i, 2)].astype(jnp.float32)
+
+    return take
+
+
+def weight_grad(turned_ref, right_ref, out_ref, before, stages, size=256):
+    count = right_ref.shape[1] // size
+    if before is not None:
+        take = staged(before, count, lambda ref, i: ref.at[:, :, at(i, size)], stages[0], stages[2])
+
+    def step(i):
+        value = dot(turned_ref[...].astype(jnp.bfloat16), right_ref[:, at(i, size)])
+        value = value.reshape(value.shape[0] // 8, 8, size)
+        if before is not None:
+            value = value + take(i)
+        out_ref[:, :, at(i, size)] = value.astype(out_ref.dtype)
+
+    tiles(count, step)
+
+
+def turn(ref, out_ref):
+    def step(i):
+        out_ref[at(i, 256)] = ref[:, at(i, 256)].T
+
+    tiles(ref.shape[1] // 256, step)
+
+
+def down_grad(ft_ref, dz_ref, out_ref, before, stages, size=256):
+    count = ft_ref.shape[0] // size
+    if before is not None:
+        take = staged(before, count, lambda ref, i: ref.at[pl.ds(i * (size // 8), size // 8)], stages[1], stages[2])
+
+    def step(i):
+        value = dot(ft_ref[at(i, size)], dz_ref[...])
+        value = value.reshape(size // 8, 8, value.shape[1])
+        if before is not None:
+            value = value + take(i)
+        out_ref[pl.ds(i * (size // 8), size // 8)] = value.astype(out_ref.dtype)
+
+    tiles(count, step)
+
+
+def backward_pass(up_ref, u_ref, qkvs, dkv_refs, gains, w, keep, work, before, stages, du_ref, gain_grads, sum_ref, ready, done):
+    before = before or dict.fromkeys(NAMES)
+    dz = up_ref
+    if up_ref.dtype != jnp.bfloat16:
+        dz = work["dz"]
+
+        def cast(i):
+            dz[at(i, 128)] = up_ref[at(i, 128)].astype(jnp.bfloat16)
+
+        tiles(up_ref.shape[0] // 128, cast)
+    ready("down")
+    dhid = work["dhid"]
+
+    def step(i):
+        value = dot_nt(dz[...], weight_rows(w["down"], i, 256)) * keep["gp"][:, at(i, 256)].astype(jnp.float32)
+        dhid[:, at(i, 256)] = value.astype(jnp.bfloat16)
+
+    tiles(w["down"].shape[0] * 8 // 256, step)
+    down_grad(keep["ft"], dz, w["down"], before["down"], stages)
+    done("down")
+    ready("up")
+    project_back(dhid, w["up"], work["dm"])
+    weight_grad(keep["bt"], dhid, w["up"], before["up"], stages)
+    done("up")
+    norm_back(keep["m"], gains[1], work["dm"], up_ref, work["dm"], work["da"], gain_grads[1])
+    ready("out")
+
+    def head_grads(i):
+        value = dot_nt(weight_rows(w["out"], i, 256), work["da"][...])
+        scale = [jnp.broadcast_to(keep["rl"][2 * i + n // 2, n % 2 : n % 2 + 1], (HEAD_DIM, value.shape[1])) for n in range(4)]
+        work["do"][at(i, 256)] = (value * jnp.concatenate(scale, 0)).astype(jnp.bfloat16)
+
+    tiles(w["out"].shape[0] * 8 // 256, head_grads)
+    weight_grad(keep["ot"], work["da"], w["out"], before["out"], stages)
+    done("out")
+    attend_back(qkvs, keep["p"], work["do"], keep["ot"], work["dqkv"], dkv_refs)
+    ready("qkv")
+    project_back(work["dqkv"], w["qkv"], du_ref)
+    weight_grad(keep["at"], work["dqkv"], w["qkv"], before["qkv"], stages)
+    done("qkv")
+    norm_back(u_ref, gains[0], du_ref, work["dm"], du_ref, None, gain_grads[0], sum_ref)
+
+
+NAMES = ("qkv", "out", "up", "down")
+KEPT = ("at", "qkv", "rl", "ot", "m", "bt", "ft", "gp")
+LOCAL = ("a", "o", "b", "f")
+WORK = ("dz", "da", "do", "dm", "dhid", "dqkv")
+
+
+def shapes_of(length, model, hidden, passes):
+    f32, bf16 = jnp.float32, jnp.bfloat16
+    shape = jax.ShapeDtypeStruct
+    pairs = model // 128
+    table = {
+        "a": shape((length, model), bf16),
+        "at": shape((model, length), bf16),
+        "qkv": shape((length, 3 * model), bf16),
+        "rl": shape((pairs, 2, length), f32),
+        "o": shape((length, model), bf16),
+        "ot": shape((model, length), f32),
+        "m": shape((length, model), f32),
+        "b": shape((length, model), bf16),
+        "bt": shape((model, length), bf16),
+        "f": shape((length, hidden), bf16),
+        "ft": shape((hidden, length), bf16),
+        "gp": shape((length, hidden), bf16),
+        "dz": shape((length, model), bf16),
+        "da": shape((length, model), bf16),
+        "do": shape((model, length), bf16),
+        "dm": shape((length, model), f32),
+        "dhid": shape((length, hidden), bf16),
+        "dqkv": shape((length, 3 * model), bf16),
+    }
+    p = [shape((pairs, 2, passes * (b + 1) * QB, QB), bf16) for b in range(length // QB)]
+    return table, p
+
+
+def scratch_of(shapes):
+    return [pltpu.VMEM(s.shape, s.dtype) for s in shapes]
+
+
+def weight_copies(hbm, vmem, sems, back=False):
+    ends = lambda n: (vmem[n], hbm[n]) if back else (hbm[n], vmem[n])
+    return {n: pltpu.make_async_copy(*ends(n), sems.at[i]) for i, n in enumerate(NAMES)}
+
+
+def forward_kernel(passes, blocks, *refs):
+    it = iter(refs)
+    u = next(it)
+    before = next(it) if passes == 2 else None
+    bias, vectors = next(it), next(it)
+    hbm = {n: next(it) for n in NAMES}
+    out = next(it)
+    keep = {n: next(it) for n in KEPT}
+    keep["p"] = [next(it) for _ in range(blocks)]
+    keep.update({n: next(it) for n in LOCAL})
+    w = {n: next(it) for n in NAMES}
+    copies = weight_copies(hbm, w, next(it))
+    for n in NAMES:
+        copies[n].start()
+    gains = [vectors[n : n + 1] for n in (1, 2)]
+    shift = vectors.at[0:1] if passes == 1 else None
+    forward_pass(u, before, bias, gains, w, keep, out, shift, lambda n: copies[n].wait())
+
+
+VMEM_LIMIT = 62 << 20
+
+
+def run_forward(u, before, bias, vectors, weights, out_dtype):
+    length, model = u.shape
+    passes = 1 if before is None else 2
+    table, p = shapes_of(length, model, weights["up"].shape[2], passes)
+    vmem, anywhere = pl.BlockSpec(memory_space=pltpu.VMEM), pl.BlockSpec(memory_space=pl.ANY)
+    inputs = [u] + ([] if before is None else [before]) + [bias, vectors]
+    out_shape = [jax.ShapeDtypeStruct((length, model), out_dtype)] + [table[n] for n in KEPT] + p
+    outs = pl.pallas_call(
+        functools.partial(forward_kernel, passes, len(p)),
+        out_shape=out_shape,
+        in_specs=[vmem] * len(inputs) + [anywhere] * 4,
+        out_specs=[vmem] * len(out_shape),
+        scratch_shapes=scratch_of([table[n] for n in LOCAL] + [weights[n] for n in NAMES]) + [pltpu.SemaphoreType.DMA((4,))],
+        name="forward%d" % passes,
+        compiler_params=pltpu.CompilerParams(vmem_limit_bytes=VMEM_LIMIT),
+    )(*inputs, *(weights[n] for n in NAMES))
+    keep = dict(zip(KEPT, outs[1:]))
+    keep["p"] = list(outs[1 + len(KEPT) :])
+    return outs[0], keep
+
+
+def backward_kernel(passes, blocks, with_before, *refs):
+    it = iter(refs)
+    up, u = next(it), next(it)
+    other = next(it)
+    vectors = next(it)
+    keep = {n: next(it) for n in KEPT}
+    keep["p"] = [next(it) for _ in range(blocks)]
+    hbm = {n: next(it) for n in NAMES}
+    before = {n: next(it) for n in NAMES} if with_before else None
+    du, ln1, ln2, whole = next(it), next(it), next(it), next(it)
+    dkv = next(it) if passes == 2 else None
+    grads = {n: next(it) for n in NAMES}
+    w = {n: next(it) for n in NAMES}
+    work = {n: next(it) for n in WORK}
+    loads, stores = weight_copies(hbm, w, next(it)), weight_copies(grads, w, next(it), back=True)
+    stages = [next(it), next(it), next(it)] if with_before else None
+    for n in reversed(NAMES):
+        loads[n].start()
+    gains = [vectors[n : n + 1] for n in (1, 2)]
+    qkvs, dkvs = ([keep["qkv"]], [other]) if passes == 1 else ([other, keep["qkv"]], [dkv, None])
+    backward_pass(
+        up, u, qkvs, dkvs, gains, w, keep, work, before, stages, du, (ln1, ln2), whole,
+        lambda n: loads[n].wait(), lambda n: stores[n].start(),
     )
-    scores = jnp.where(allowed[None], scores, -1e30)
-    peak = jnp.max(scores, -1, keepdims=True)
-    expos = jnp.exp(scores - peak)
-    probs = expos / jnp.sum(expos, -1, keepdims=True)
-    attn = jnp.einsum(
-        "hqk,khd->qhd", probs.astype(jnp.bfloat16), value_rows, preferred_element_type=jnp.float32
+    for n in NAMES:
+        stores[n].wait()
+
+
+def run_backward(up, u, other, vectors, keep, weights, before, passes):
+    length, model = u.shape
+    f32, bf16 = jnp.float32, jnp.bfloat16
+    shape = jax.ShapeDtypeStruct
+    table, p = shapes_of(length, model, weights["up"].shape[2], passes)
+    vmem, anywhere = pl.BlockSpec(memory_space=pltpu.VMEM), pl.BlockSpec(memory_space=pl.ANY)
+    inputs = [up, u, other, vectors] + [keep[n] for n in KEPT] + keep["p"]
+    far = [weights[n] for n in NAMES] + ([] if before is None else [before[n] for n in NAMES])
+    out_shape = [shape((length, model), f32)] + [shape((8, model), f32)] * 3
+    if passes == 2:
+        out_shape.append(shape((length, 2 * model), f32))
+    near = len(out_shape)
+    out_shape += [shape(weights[n].shape, bf16) for n in NAMES]
+    scratch = scratch_of([weights[n] for n in NAMES] + [table[n] for n in WORK])
+    scratch += [pltpu.SemaphoreType.DMA((4,)), pltpu.SemaphoreType.DMA((4,))]
+    if before is not None:
+        scratch += [
+            pltpu.VMEM((2, model // 8, 8, 256), bf16),
+            pltpu.VMEM((2, 32, 8, model), bf16),
+            pltpu.SemaphoreType.DMA((2,)),
+        ]
+    outs = pl.pallas_call(
+        functools.partial(backward_kernel, passes, len(p), before is not None),
+        out_shape=out_shape,
+        in_specs=[vmem] * len(inputs) + [anywhere] * len(far),
+        out_specs=[vmem] * near + [anywhere] * 4,
+        scratch_shapes=scratch,
+        name="backward%d" % passes,
+        compiler_params=pltpu.CompilerParams(vmem_limit_bytes=VMEM_LIMIT),
+    )(*inputs, *far)
+    return outs[:near], dict(zip(NAMES, outs[near:]))
+
+
+AXES = ("dp", "fsdp")
+
+
+def cut(w):
+    return w.reshape(w.shape[0] // 8, 8, w.shape[1])
+
+
+def join(w):
+    return w.reshape(w.shape[0] * 8, w.shape[2])
+
+
+def gather_weights(near, vectors, shards):
+    if not near:
+        vectors = [lax.all_gather(v, AXES, axis=0, tiled=True) for v in vectors]
+        weights = {n: cut(lax.all_gather(shards[n], AXES, axis=0, tiled=True)) for n in NAMES}
+        return jnp.stack(vectors).astype(jnp.float32), weights
+    rows = vectors[0].shape[0]
+    small = jnp.zeros((1, 8, 128), jnp.bfloat16).at[0, :3, :rows].set(jnp.stack(vectors))
+    small, *wholes = gather_all([small] + [cut(shards[n]) for n in ("out", "qkv", "up", "down")])
+    vectors = small[:, :3, :rows].transpose(1, 0, 2).reshape(3, 32 * rows)
+    return vectors.astype(jnp.float32), dict(zip(("out", "qkv", "up", "down"), wholes))
+
+
+def reduce_grads(near, vectors, grads):
+    if not near:
+        vectors = [lax.psum_scatter(v, AXES, scatter_dimension=0, tiled=True) for v in vectors]
+        return vectors, {n: lax.psum_scatter(join(grads[n]).astype(jnp.float32), AXES, scatter_dimension=0, tiled=True) for n in NAMES}
+    rows = vectors[0].shape[0] // 32
+    small = jnp.stack(vectors).reshape(3, 32, rows).transpose(1, 0, 2)
+    small = jnp.zeros((32, 8, 128), jnp.bfloat16).at[:, :3, :rows].set(small.astype(jnp.bfloat16))
+    order = ("down", "up", "out", "qkv")
+    *sums, small = reduce_all([grads[n] for n in order] + [small])
+    return [small[0, n, :rows] for n in range(3)], {n: join(s) for n, s in zip(order, sums)}
+
+
+def body(near, tokens, doc_ids, pass_embed, ln1_gain, w_qkv, w_out, ln2_gain, w_up, w_down, cotangent):
+    shards = {"qkv": w_qkv, "out": w_out, "up": w_up, "down": w_down}
+    vectors, weights = gather_weights(near, (pass_embed, ln1_gain, ln2_gain), shards)
+    vectors = jnp.pad(vectors, ((0, 5), (0, 0)))
+    length = tokens.shape[0]
+    at_ = jnp.arange(length, dtype=jnp.int32)
+    allowed = (doc_ids[:, None] == doc_ids[None, :]) & (at_[:, None] <= at_[None, :])
+    bias = jnp.where(allowed, 0.0, -1e30).astype(jnp.float32)
+    second_in, kept1 = run_forward(tokens, None, bias, vectors, weights, jnp.float32)
+    layer_out, kept2 = run_forward(second_in, kept1["qkv"], bias, vectors, weights, jnp.bfloat16)
+    (second_g, late1, late2, embed_g, dkv), late = run_backward(
+        cotangent, second_in, kept1["qkv"], vectors, kept2, weights, None, 2
     )
-    attn = attn.astype(jnp.bfloat16).reshape(length, model_width)
-    middle = inputs + jnp.dot(attn, out_w, preferred_element_type=jnp.float32)
-    second = layer_norm(middle, ln2_w.astype(jnp.float32)).astype(jnp.bfloat16)
-    hidden = jnp.dot(second, up_w, preferred_element_type=jnp.float32)
-    active = exact_gelu(hidden).astype(jnp.bfloat16)
-    result = middle + jnp.dot(active, down_w, preferred_element_type=jnp.float32)
-    kept = {
-        "normed": normed,
-        "queries": queries,
-        "key_rows": key_rows,
-        "value_rows": value_rows,
-        "probs": probs,
-        "attn": attn,
-        "middle": middle,
-        "second": second,
-        "hidden": hidden,
-        "active": active,
-        "own_kv": (own_keys, own_values),
-    }
-    return (result, kept)
-
-
-def run_back(inputs, earlier, allowed, weights, upstream, extra):
-    embed, ln1_w, qkv_w, out_w, ln2_w, up_w, down_w = weights
-    length, model_width = inputs.shape
-    head_count = model_width // HEAD_DIM
-    scale = HEAD_DIM ** (-0.5)
-    unused, kept = run_block(inputs, earlier, allowed, weights)
-    down_rounded = upstream.astype(jnp.bfloat16)
-    down_g = jnp.dot(kept["active"].T, down_rounded, preferred_element_type=jnp.float32)
-    active_g = jnp.dot(down_rounded, down_w.T, preferred_element_type=jnp.float32)
-    unused_gelu, gelu_pull = jax.vjp(exact_gelu, kept["hidden"])
-    hidden_g = gelu_pull(active_g)[0].astype(jnp.bfloat16)
-    up_g = jnp.dot(kept["second"].T, hidden_g, preferred_element_type=jnp.float32)
-    second_g = jnp.dot(hidden_g, up_w.T, preferred_element_type=jnp.float32)
-    unused_norm, norm_pull = jax.vjp(layer_norm, kept["middle"], ln2_w.astype(jnp.float32))
-    middle_part, ln2_g = norm_pull(second_g)
-    middle_g = upstream + middle_part
-    attn_rounded = middle_g.astype(jnp.bfloat16)
-    wout_g = jnp.dot(kept["attn"].T, attn_rounded, preferred_element_type=jnp.float32)
-    attn_g = jnp.dot(attn_rounded, out_w.T, preferred_element_type=jnp.float32)
-    attn_g = attn_g.astype(jnp.bfloat16).reshape(length, head_count, HEAD_DIM)
-    probs = kept["probs"]
-    value_g = jnp.einsum(
-        "hqk,qhd->khd", probs.astype(jnp.bfloat16), attn_g, preferred_element_type=jnp.float32
-    )
-    probs_g = jnp.einsum(
-        "qhd,khd->hqk", attn_g, kept["value_rows"], preferred_element_type=jnp.float32
-    )
-    scores_g = probs * (probs_g - jnp.sum(probs * probs_g, -1, keepdims=True))
-    scores_g = scores_g.astype(jnp.bfloat16)
-    query_g = (
-        jnp.einsum("hqk,khd->qhd", scores_g, kept["key_rows"], preferred_element_type=jnp.float32)
-        * scale
-    )
-    key_g = (
-        jnp.einsum("hqk,qhd->khd", scores_g, kept["queries"], preferred_element_type=jnp.float32)
-        * scale
-    )
-    if earlier is None:
-        earlier_g = None
-        own_key_g, own_value_g = (key_g, value_g)
-    else:
-        earlier_g = (key_g[:length], value_g[:length])
-        own_key_g, own_value_g = (key_g[length:], value_g[length:])
-    if extra is not None:
-        own_key_g = own_key_g + extra[0]
-        own_value_g = own_value_g + extra[1]
-    qkv_rounded = jnp.stack([query_g, own_key_g, own_value_g], 1).astype(jnp.bfloat16)
-    qkv_rounded = qkv_rounded.reshape(length, 3 * model_width)
-    qkv_g = jnp.dot(kept["normed"].T, qkv_rounded, preferred_element_type=jnp.float32)
-    normed_g = jnp.dot(qkv_rounded, qkv_w.T, preferred_element_type=jnp.float32)
-    unused_first, first_pull = jax.vjp(layer_norm, inputs, ln1_w.astype(jnp.float32))
-    input_part, ln1_g = first_pull(normed_g)
-    input_g = middle_g + input_part
-    return ((ln1_g, qkv_g, wout_g, ln2_g, up_g, down_g), input_g, earlier_g)
-
-
-AXES = ("dp", "fsdp")
-
-
-def gather_weights(near, shards):
-    if not near:
-        return tuple(lax.all_gather(s, AXES, axis=0, tiled=True) for s in shards)
-    embed, ln1, qkv, out, ln2, up, down = shards
-    rows = embed.shape[0]
-    small = jnp.zeros((1, 8, 128), jnp.bfloat16)
-    small = small.at[0, :3, :rows].set(jnp.stack([embed, ln1, ln2]))
-    cut = lambda w: w.reshape(w.shape[0] // 8, 8, w.shape[1])
-    small, out, qkv, up, down = gather_all([small, cut(out), cut(qkv), cut(up), cut(down)])
-    vectors = small[:, :3, :rows].transpose(1, 0, 2).reshape(3, 32 * rows)
-    join = lambda w: w.reshape(w.shape[0] * 8, w.shape[2])
-    return (vectors[0], vectors[1], join(qkv), join(out), vectors[2], join(up), join(down))
-
-
-def reduce_grads(near, totals):
-    if not near:
-        return lax.psum_scatter(totals, AXES, scatter_dimension=0, tiled=True)
-    embed, ln1, qkv, out, ln2, up, down = totals
-    rows = embed.shape[0] // 32
-    small = jnp.stack([embed, ln1, ln2]).reshape(3, 32, rows).transpose(1, 0, 2)
-    small = jnp.zeros((32, 8, 128), jnp.bfloat16).at[:, :3, :rows].set(small.astype(jnp.bfloat16))
-    cut = lambda w: w.astype(jnp.bfloat16).reshape(w.shape[0] // 8, 8, w.shape[1])
-    down, up, out, qkv, small = reduce_all([cut(down), cut(up), cut(out), cut(qkv), small])
-    join = lambda w: w.reshape(w.shape[0] * 8, w.shape[2])
-    return (small[0, 0, :rows], small[0, 1, :rows], join(qkv), join(out), small[0, 2, :rows], join(up), join(down))
-
-
-def body(near, tokens, doc_ids, pass_embed, ln1_gain, w_qkv, w_out, ln2_gain, w_up, w_down, cotangent):
-    weights = gather_weights(near, (pass_embed, ln1_gain, w_qkv, w_out, ln2_gain, w_up, w_down))
-    length = tokens.shape[0]
-    places = jnp.arange(length, dtype=jnp.int32)
-    allowed = (doc_ids[:, None] == doc_ids[None, :]) & (places[None, :] <= places[:, None])
-    doubled = jnp.concatenate([allowed, allowed], 1)
-    inputs = tokens.astype(jnp.float32)
-    first_out, first_kept = run_block(inputs, None, allowed, weights)
-    earlier = first_kept["own_kv"]
-    second_in = first_out + weights[0].astype(jnp.float32)
-    second_out, unused = run_block(second_in, earlier, doubled, weights)
-    layer_out = second_out.astype(jnp.bfloat16)
-    late_grads, second_in_g, earlier_g = run_back(
-        second_in, earlier, doubled, weights, cotangent.astype(jnp.float32), None
-    )
-    embed_g = jnp.sum(second_in_g, 0)
-    early_grads, tokens_grad, unused_g = run_back(
-        inputs, None, allowed, weights, second_in_g, earlier_g
-    )
-    totals = (embed_g,) + tuple((a + b for a, b in zip(late_grads, early_grads)))
-    return (layer_out, tokens_grad, *reduce_grads(near, totals))
+    (tokens_grad, early1, early2, _), grads = run_backward(second_g, tokens, dkv, vectors, kept1, weights, late, 1)
+    small, sums = reduce_grads(near, (embed_g[0], late1[0] + early1[0], late2[0] + early2[0]), grads)
+    return (layer_out, tokens_grad, small[0], small[1], sums["qkv"], sums["out"], small[2], sums["up"], sums["down"])
 
 
 def solution(mesh):

time: 512 us -> 384 us (0.75)
  matrix products: 219 us -> 0 us
  Pallas kernels: 177 us -> 368 us
  other arithmetic: 73 us -> 4.9 us
  local copies, waits for them, and re-layouts: 37.7 us -> 10.3 us
    dot_general x35 -> x0, matrix products: 211 us -> none  [the longest x2 40.1 us: run_block(): hidden = jnp.dot(second, up_w, preferred_element_type=jnp.float32)]
    pallas_call x0 -> x4, Pallas kernels: none -> 191 us  [the longest x2 110 us: run_backward(): pl.pallas_call(functools.partial(backward_kernel, passes, len(p), before...]
    sub x1 -> x0, other arithmetic: 33.3 us -> none  [run_block(): expos = jnp.exp(scores - peak)]
    convert_element_type x6 -> x0, other arithmetic: 29.8 us -> none  [the longest x2 28.9 us: run_back(): scores_g = scores_g.astype(jnp.bfloat16)]
    convert_element_type x7 -> x3, local copies, waits for them, and re-layouts: 12.2 us -> 0.95 us  [gather_weights(): vectors.astype(jnp.float32)]
    unnamed x182 -> x4, local copies, waits for them, and re-layouts: 17.5 us -> 6.54 us
    sub x1 -> x0, matrix products: 7.51 us -> none  [run_block(): expos = jnp.exp(scores - peak)]
    reduce_sum x10 -> x0, other arithmetic: 6.76 us -> none  [the longest x4 3.2 us: layer_norm(): center = values - jnp.mean(values, -1, keepdims=True)]
where the time goes in v2:
time: 384 us; the launch traced here: 383 us
  Pallas kernels  368 us (96%)
  local copies, waits for them, and re-layouts  10.3 us (3%)
  other arithmetic  4.9 us (1%)
    pallas_call x2, Pallas kernels, run_backward(): pl.pallas_call(functools.partial(backward_kernel, passes, len(p), before...  110 us
    pallas_call x1, Pallas kernels, reduce_all(): pl.pallas_call(functools.partial(reduce_kernel, count), out_shape=[jax.Sh...  94.2 us
    pallas_call x1, Pallas kernels, gather_all(): pl.pallas_call(gather_kernel, out_shape=[jax.ShapeDtypeStruct((32 * s.sha...  82.7 us
    pallas_call x2, Pallas kernels, run_forward(): pl.pallas_call(functools.partial(forward_kernel, passes, len(p)), out_sha...  80.4 us

profile of v2, /device:TPU:0, one launch (start us, length us, event | category | flops | bytes accessed | tf_op | source)
XLA Modules:
  0.0 383.5 jit_solution(474473196647252272)
XLA Ops:
  0.6 0.7 maximum_bitcast_fusion.1
  1.3 0.6 scatter.6.refs_0_
  1.9 1.9 fusion.1.refs_1_.refs_2_
  3.9 82.7 %gather.1 = (bf16[32,8,128]{2,1,0:T(8,128)(2,1)}, bf16[96,8,768]{2,1,0:T(8,128)(2,1)}, bf16[96,8,2304]{2,1,0:T(8,128)(2,1)}, bf16[96,8,3072]{2,1,0:T(8,128)(2,1)}, bf16[384,8,768]{2,1,0:T(8,128)(2,1)}) custom-call(bf16[1,8,128]{2,1,0:T(8,128)(2,1)} %scatter.6.refs_0_, bf16[3,8,768]{2,1,0:T(8,128)(2,1)} %bitcast.30, bf16[3,8,2304]{2,1,0:T(8,128)(2,1)} %bitcast.28, ...), custom_call_target="tpu_custom_call" | custom-call | tf_op jit(solution)/shard_map/gather/pallas_call | solution.py:154
  86.6 0.9 slice_bitcast_fusion
  87.5 0.1 convert_element_type.14
  87.6 0.6 pad_convert_fusion.refs_2_.refs_3_
  88.2 37.2 %forward1.1 = (f32[512,768]{1,0:T(8,128)}, bf16[768,512]{1,0:T(8,128)(2,1)}, bf16[512,2304]{1,0:T(8,128)(2,1)}, f32[6,2,512]{2,1,0:T(2,128)}, f32[768,512]{1,0:T...) custom-call(bf16[512,768]{1,0:T(8,128)(2,1)} %refs_1_.1, ...), custom_call_target="tpu_custom_call" | custom-call | tf_op jit(solution)/shard_map/forward1/pallas_call | solution.py:703
  125.4 43.2 %forward2.1 = (bf16[512,768]{1,0:T(8,128)(2,1)}, bf16[768,512]{1,0:T(8,128)(2,1)}, bf16[512,2304]{1,0:T(8,128)(2,1)}, f32[6,2,512]{2,1,0:T(2,128)}, f32[768,512]...) custom-call(f32[512,768]{1,0:T(8,128)} %get-tuple-element.86.refs_0_, ...), custom_call_target="tpu_custom_call" | custom-call | tf_op jit(solution)/shard_map/forward2/pallas_call | solution.py:703
  168.6 54.4 %backward2.1 = (f32[512,768]{1,0:T(8,128)}, f32[8,768]{1,0:T(8,128)}, f32[8,768]{1,0:T(8,128)}, f32[8,768]{1,0:T(8,128)}, f32[512,1536]{1,0:T(8,128)}, /*index=5...) custom-call(bf16[512,768]{1,0:T(8,128)(2,1)} %refs_0_.3, ...), custom_call_target="tpu_custom_call" | custom-call | tf_op jit(solution)/shard_map/backward2/pallas_call | solution.py:766
  223.0 55.8 %backward1.1 = (f32[512,768]{1,0:T(8,128)}, f32[8,768]{1,0:T(8,128)}, f32[8,768]{1,0:T(8,128)}, f32[8,768]{1,0:T(8,128)}, bf16[96,8,2304]{2,1,0:T(8,128)(2,1)}, ...) custom-call(f32[512,768]{1,0:T(8,128)} %get-tuple-element.99.refs_0_, ...), custom_call_target="tpu_custom_call" | custom-call | tf_op jit(solution)/shard_map/backward1/pallas_call | solution.py:766
  278.8 0.8 fusion.2
  279.6 0.8 convert_reduce_fusion.1
  280.4 0.1 stack.32
  280.5 0.1 stack.31
  280.6 0.1 stack.33
  280.7 0.1 maximum_bitcast_fusion
  280.8 0.7 scatter.9.refs_4_
  281.4 94.2 %reduce.11 = (f32[12,8,768]{2,1,0:T(8,128)}, f32[3,8,3072]{2,1,0:T(8,128)}, f32[3,8,768]{2,1,0:T(8,128)}, f32[3,8,2304]{2,1,0:T(8,128)}, f32[1,8,128]{2,1,0:T(8,128)}) custom-call(bf16[384,8,768]{2,1,0:T(8,128)(2,1)} %get-tuple-element.115.refs_0_, bf16[96,8,3072]{2,1,0:T(8,128)(2,1)} %get-tuple-element.116.refs_1_, ...), custom_call_target="tpu_custom_call" | custom-call | tf_op jit(solution)/shard_map/reduce/pallas_call | solution.py:291
  375.6 1.3 slice_bitcast_fusion.1
  376.9 1.6 copy.28
  378.6 1.5 copy.29
  380.1 1.7 copy.30
  381.8 1.7 copy.31
  (1 shorter events, 0.0 us)

commit v3 on v2

v3 whole, which is shorter than its diff:
```python
import functools
import math

import jax
import jax.numpy as jnp
from jax import lax
from jax.experimental import pallas as pl
from jax.experimental.pallas import tpu as pltpu
from jax.sharding import PartitionSpec as P

HEAD_DIM = 64


MESH = pl.DeviceIdType.MESH
NAMES = ("qkv", "out", "up", "down")


def pieces(width, parts):
    count = width // 128 // parts
    result = []
    for n in range(parts):
        first = (count + 1 - n % 2) // 2
        start = n * count * 128
        result.append(((start, first * 128), (start + first * 128, (count - first) * 128)))
    return result


class Links:
    def __init__(self, chunks, depth):
        d, z = lax.axis_index("dp"), lax.axis_index("fsdp")
        y, x, c = d // 4, lax.rem(d // 2, 2), lax.rem(d, 2)
        self.d, self.z, self.y, self.x, self.c = d, z, y, x, c
        self.sideways = (y * 4 + (1 - x) * 2 + c, z)
        self.upward = ((1 - y) * 4 + x * 2 + c, z)
        self.sibling = (y * 4 + x * 2 + 1 - c, z)
        self.along = [(d, lax.rem(z + k, 4)) for k in (1, 2, 3)]
        self.chunks, self.depth = chunks, depth

    def greet(self):
        peers = [self.sideways, self.upward, self.sibling, *self.along]
        barrier = pltpu.get_barrier_semaphore()
        for peer in peers:
            pl.semaphore_signal(barrier, inc=1, device_id=peer, device_id_type=MESH)
        pl.semaphore_wait(barrier, len(peers))

    def columns(self, n):
        halves = self.chunks[n][1]
        return pl.ds(halves[0][0], sum(size for _, size in halves))

    def rows(self, n):
        return self.depth[self.chunks[n][0]]

    def hops(self, h):
        return (self.sideways, self.upward) if h == 0 else (self.upward, self.sideways)


def remote(src, dst, send, recv, peer):
    return pltpu.make_async_remote_copy(
        src_ref=src, dst_ref=dst, send_sem=send, recv_sem=recv, device_id=peer, device_id_type=MESH
    )


def link_semaphores(count):
    dma = pltpu.SemaphoreType.DMA
    return [dma((count, 3)), dma((count, 3)), dma((count, 2, 3)), dma((count, 2, 3)), dma((count, 4)), dma((count, 4)), dma((count,))]


class Gather:
    def __init__(self, chunks, shards, wholes, sems):
        self.links = Links(chunks, {n: s.shape[0] for n, s in shards.items()})
        self.chunks, self.shards, self.wholes = chunks, shards, wholes
        self.z_send, self.z_recv, self.p_send, self.p_recv, self.d_send, self.d_recv, self.own_sem = sems

    def group(self, n, y, x, cols):
        rows = self.links.rows(n)
        return self.wholes[self.chunks[n][0]].at[pl.ds((y * 4 + x * 2 + self.links.c) * 4 * rows, 4 * rows), :, cols]

    def near(self, n):
        rows, cols = self.links.rows(n), self.links.columns(n)
        name = self.chunks[n][0]
        at = (self.links.d * 4 + self.links.z) * rows
        return self.shards[name].at[:, :, cols], self.wholes[name].at[pl.ds(at, rows), :, cols]

    def own(self, n):
        return pltpu.make_async_copy(*self.near(n), self.own_sem.at[n])

    def ahead(self, n, k):
        return remote(*self.near(n), self.z_send.at[n, k], self.z_recv.at[n, k], self.links.along[k])

    def hop(self, n, h, i):
        at = self.links
        one, two = at.hops(h)
        y, x = at.y, at.x
        if i == 2:
            y, x = (y, 1 - x) if h == 0 else (1 - y, x)
        block = self.group(n, y, x, pl.ds(*self.chunks[n][1][h]))
        return remote(block, block, self.p_send.at[n, h, i], self.p_recv.at[n, h, i], one if i == 0 else two)

    def share(self, n, g):
        at = self.links
        y, x = at.y, at.x
        block = self.group(n, 1 - y if g >= 2 else y, 1 - x if g % 2 else x, at.columns(n))
        return remote(block, block, self.d_send.at[n, g], self.d_recv.at[n, g], at.sibling)

    def halves(self, n):
        return range(len(self.chunks[n][1]))

    def step(self, what, n):
        if what == "begin":
            self.own(n).start()
            for k in range(3):
                self.ahead(n, k).start()
        elif what == "first":
            self.own(n).wait()
            for k in range(3):
                self.ahead(n, k).wait_recv()
            for h in self.halves(n):
                self.hop(n, h, 0).start()
                self.hop(n, h, 1).start()
            self.share(n, 0).start()
        elif what == "second":
            for h in self.halves(n):
                self.hop(n, h, 0).wait_recv()
                self.hop(n, h, 2).start()
        elif what == "third":
            for h in self.halves(n):
                self.hop(n, h, 1).wait_recv()
            self.share(n, 1).start()
            self.share(n, 2).start()
        elif what == "fourth":
            for h in self.halves(n):
                self.hop(n, h, 2).wait_recv()
            self.share(n, 3).start()
        elif what == "finish":
            for g in range(4):
                self.share(n, g).wait_recv()
        elif what == "close":
            for k in range(3):
                self.ahead(n, k).wait_send()
            for h in self.halves(n):
                for i in range(3):
                    self.hop(n, h, i).wait_send()
            for g in range(4):
                self.share(n, g).wait_send()


def staggered(count, ahead, stages):
    events = [("begin", n) for n in range(min(ahead, count))]
    for tick in range(count + len(stages) - 1):
        for late, what in enumerate(stages):
            if 0 <= tick - late < count:
                events.append((what, tick - late))
                if late == 0 and tick + ahead < count:
                    events.append(("begin", tick + ahead))
    return events


class Pump:
    def __init__(self, step, events):
        self.run, self.events, self.next = step, events, 0

    def take(self, count):
        taken = self.events[self.next : self.next + count]
        self.next += len(taken)
        return taken

    def until(self, *event):
        if event in self.events[self.next :]:
            for one in self.take(self.events.index(event) + 1 - self.next):
                self.run(*one)

    def rest(self):
        for one in self.take(len(self.events)):
            self.run(*one)

    def hook(self, loops, count):
        plan = [self.take(count * (i + 1) // loops - count * i // loops) for i in range(loops)]

        def at_step(i):
            for k, events in enumerate(plan):
                if events:

                    @pl.when(i == k)
                    def _(events=events):
                        for one in events:
                            self.run(*one)

        return at_step


class Reduce:
    def __init__(self, chunks, parts, r0, r1, r2, r3, outs, sems):
        self.links = Links(chunks, {n: s.shape[0] for n, s in outs.items()})
        self.chunks, self.parts, self.outs = chunks, parts, outs
        self.r0, self.r1, self.r2, self.r3 = r0, r1, r2, r3
        self.z_send, self.z_recv, self.p_send, self.p_recv, self.d_send, self.d_recv, _ = sems

    def share(self, n, g):
        at, name = self.links, self.chunks[n][0]
        span, cols = 4 * at.rows(n), at.columns(n)
        src = self.parts[name].at[pl.ds((g * 2 + 1 - at.c) * span, span), :, cols]
        dst = self.r0[name].at[pl.ds(g * span, span), :, cols]
        return remote(src, dst, self.d_send.at[n, g], self.d_recv.at[n, g], at.sibling)

    def hop(self, n, h, i):
        at, name = self.links, self.chunks[n][0]
        span, cols = 4 * at.rows(n), pl.ds(*self.chunks[n][1][h])
        two, one = at.hops(h)
        if i < 2:
            g = (1 - at.y) * 2 + i if h == 0 else i * 2 + 1 - at.x
            src = self.r0[name].at[pl.ds(g * span, span), :, cols]
            dst = self.r1[name].at[pl.ds(i * span, span), :, cols]
        else:
            far = 1 - at.x if h == 0 else 1 - at.y
            src = self.r1[name].at[pl.ds(far * span, span), :, cols]
            dst = self.r2[name].at[:, :, cols]
        return remote(src, dst, self.p_send.at[n, h, i], self.p_recv.at[n, h, i], one if i < 2 else two)

    def ahead(self, n, k):
        at, name = self.links, self.chunks[n][0]
        rows, cols = at.rows(n), at.columns(n)
        src = self.r2[name].at[pl.ds(lax.rem(at.z + k + 1, 4) * rows, rows), :, cols]
        dst = self.r3[name].at[pl.ds(k * rows, rows), :, cols]
        return remote(src, dst, self.z_send.at[n, k], self.z_recv.at[n, k], at.along[k])

    def add(self, count, into, into_at, other, other_at, cols):
        def one(i, carry):
            into[into_at + i, :, cols] = (
                into[into_at + i, :, cols].astype(jnp.float32) + other[other_at + i, :, cols].astype(jnp.float32)
            ).astype(into.dtype)
            return carry

        lax.fori_loop(0, count, one, 0)

    def halves(self, n):
        return range(len(self.chunks[n][1]))

    def step(self, what, n):
        at, name = self.links, self.chunks[n][0]
        rows = at.rows(n)
        span = 4 * rows
        if what == "begin":
            for g in range(4):
                self.share(n, g).start()
        elif what == "first":
            for g in range(4):
                self.share(n, g).wait_recv()
                self.add(span, self.r0[name], g * span, self.parts[name], (g * 2 + at.c) * span, at.columns(n))
            for h in self.halves(n):
                self.hop(n, h, 0).start()
                self.hop(n, h, 1).start()
        elif what == "second":
            for h in self.halves(n):
                cols = pl.ds(*self.chunks[n][1][h])
                for i in range(2):
                    self.hop(n, h, i).wait_recv()
                    g = at.y * 2 + i if h == 0 else i * 2 + at.x
                    self.add(span, self.r1[name], i * span, self.r0[name], g * span, cols)
                self.hop(n, h, 2).start()
        elif what == "third":
            for h in self.halves(n):
                cols = pl.ds(*self.chunks[n][1][h])
                self.hop(n, h, 2).wait_recv()
                self.add(span, self.r2[name], 0, self.r1[name], (at.x if h == 0 else at.y) * span, cols)
            for k in range(3):
                self.ahead(n, k).start()
        elif what == "finish":
            cols = at.columns(n)
            for k in range(3):
                self.ahead(n, k).wait_recv()

            def one(i, carry):
                total = self.r2[name][at.z * rows + i, :, cols].astype(jnp.float32)
                for k in range(3):
                    total = total + self.r3[name][k * rows + i, :, cols].astype(jnp.float32)
                self.outs[name][i, :, cols] = total
                return carry

            lax.fori_loop(0, rows, one, 0)
        elif what == "close":
            for g in range(4):
                self.share(n, g).wait_send()
            for h in self.halves(n):
                for i in range(3):
                    self.hop(n, h, i).wait_send()
            for k in range(3):
                self.ahead(n, k).wait_send()


EPS = 1e-05
QB = 256
SCALE = HEAD_DIM ** (-0.5)
NT = (((1,), (1,)), ((), ()))


def dot(left, right):
    return jnp.dot(left, right, preferred_element_type=jnp.float32)


def dot_nt(left, right):
    return lax.dot_general(left, right, NT, preferred_element_type=jnp.float32)


def tiles(count, step):
    def one(i, carry):
        step(i)
        return carry

    lax.fori_loop(0, count, one, 0)


def at(i, size):
    return pl.ds(pl.multiple_of(i * size, size), size)


def weight_columns(w, i, size):
    block = w[:, :, at(i, size)]
    return block.reshape(block.shape[0] * 8, size)


def weight_rows(w, i, size):
    block = w[pl.ds(i * (size // 8), size // 8)]
    return block.reshape(size, block.shape[2])


def normal(u):
    center = u - jnp.mean(u, -1, keepdims=True)
    spread = lax.rsqrt(jnp.mean(center * center, -1, keepdims=True) + EPS)
    return center * spread, spread


def norm_rows(u_ref, gain, out_ref):
    def step(i):
        hat, spread = normal(u_ref[at(i, 128)].astype(jnp.float32))
        out_ref[at(i, 128)] = (hat * gain).astype(jnp.bfloat16)

    tiles(u_ref.shape[0] // 128, step)


def gelu_both(x):
    e = jnp.exp(x * x * -0.5)
    t = 1.0 / (1.0 + jnp.abs(x) * (0.3275911 * 0.5**0.5))
    poly = 0.5 * 1.061405429
    for term in (-1.453152027, 1.421413741, -0.284496736, 0.254829592):
        poly = poly * t + 0.5 * term
    tail = poly * t * e
    cdf = jnp.where(x >= 0, 1.0 - tail, tail)
    return x * cdf, cdf + x * e * (0.5 / math.pi) ** 0.5


def split_heads(block, axis):
    half = lax.broadcasted_iota(jnp.int32, block.shape, axis) < HEAD_DIM
    zero = jnp.zeros_like(block)
    return jnp.where(half, block, zero), jnp.where(half, zero, block)


def attend(qkvs, bias_ref, p_refs, rl_ref, o_ref, ot_ref, hook=None):
    model = o_ref.shape[1]
    own = qkvs[-1]

    def step(pair):
        if hook is not None:
            hook(pair)
        lanes = at(pair, 128)
        keys, values = [], []
        for ref in qkvs:
            keys.append(ref[:, pl.ds(pl.multiple_of(model + pair * 128, 128), 128)])
            values.append(ref[:, pl.ds(pl.multiple_of(2 * model + pair * 128, 128), 128)].T)
        for b in range(own.shape[0] // QB):
            span = (b + 1) * QB
            queries = split_heads(own[b * QB : span, lanes] * SCALE, 1)
            bias = bias_ref[:span, b * QB : span]
            halves = []
            for h in range(2):
                scores = [dot_nt(k[:span], queries[h]) + bias for k in keys]
                peak = jnp.max(scores[0], 0, keepdims=True)
                for s in scores[1:]:
                    peak = jnp.maximum(peak, jnp.max(s, 0, keepdims=True))
                total, out = None, None
                for n, s in enumerate(scores):
                    p = jnp.exp(s - peak)
                    part = jnp.sum(p, 0, keepdims=True)
                    p = p.astype(jnp.bfloat16)
                    p_refs[b][pair, h, n * span : (n + 1) * span] = p
                    product = dot(values[n][h * HEAD_DIM : (h + 1) * HEAD_DIM, :span], p)
                    total = part if total is None else total + part
                    out = product if out is None else out + product
                scale = 1.0 / total
                rl_ref[pair, h : h + 1, b * QB : span] = scale
                halves.append(out * scale)
            both = jnp.concatenate(halves, 0)
            ot_ref[at(pair, 128), b * QB : span] = both
            o_ref[b * QB : span, lanes] = both.astype(jnp.bfloat16).T

    tiles(model // 128, step)


def attend_back(qkvs, p_refs, do_ref, ot_ref, dqkv_ref, dkv_refs, hook=None):
    model = do_ref.shape[0]
    own = qkvs[-1]

    def step(pair):
        if hook is not None:
            hook(pair)
        lanes = at(pair, 128)
        rows = at(pair, 128)
        right = [pl.ds(pl.multiple_of(n * model + pair * 128, 128), 128) for n in range(3)]
        keys = [ref[:, right[1]] for ref in qkvs]
        values = [ref[:, right[2]] for ref in qkvs]
        turned = [k.T for k in keys]
        dk, dv = [None] * len(qkvs), [None] * len(qkvs)
        for b in reversed(range(own.shape[0] // QB)):
            span = (b + 1) * QB
            block = slice(b * QB, span)
            queries = split_heads(own[block, lanes] * SCALE, 1)
            do = do_ref[rows, block]
            do_down = split_heads(do, 0)
            do_across = split_heads(do.T, 1)
            product = do.astype(jnp.float32) * ot_ref[rows, block]
            dq = []
            for h in range(2):
                delta = jnp.sum(product[h * HEAD_DIM : (h + 1) * HEAD_DIM], 0, keepdims=True)
                dq_head = None
                for n in range(len(qkvs)):
                    p = p_refs[b][pair, h, n * span : (n + 1) * span]
                    ds = dot(values[n][:span], do_down[h]) - delta
                    ds = (p.astype(jnp.float32) * ds).astype(jnp.bfloat16)
                    more_dv, more_dk = dot(p, do_across[h]), dot(ds, queries[h])
                    more_dq = dot(turned[n][h * HEAD_DIM : (h + 1) * HEAD_DIM, :span], ds)
                    dq_head = more_dq if dq_head is None else dq_head + more_dq
                    if dk[n] is None:
                        dk[n], dv[n] = more_dk, more_dv
                    elif dk[n].shape[0] == span:
                        dk[n], dv[n] = dk[n] + more_dk, dv[n] + more_dv
                    else:
                        dk[n] = jnp.concatenate([dk[n][:span] + more_dk, dk[n][span:]], 0)
                        dv[n] = jnp.concatenate([dv[n][:span] + more_dv, dv[n][span:]], 0)
                dq.append(dq_head)
            dq = (jnp.concatenate(dq, 0) * SCALE).astype(jnp.bfloat16)
            dqkv_ref[block, lanes] = dq.T
        for n, ref in enumerate(dkv_refs):
            if ref is not None and n < len(qkvs) - 1:
                ref[:, lanes] = dk[n]
                ref[:, right[1]] = dv[n]
        extra = dkv_refs[-1]
        dk, dv = dk[-1], dv[-1]
        if extra is not None:
            dk, dv = dk + extra[:, lanes], dv + extra[:, right[1]]
        dqkv_ref[:, right[1]] = dk.astype(jnp.bfloat16)
        dqkv_ref[:, right[2]] = dv.astype(jnp.bfloat16)

    tiles(model // 128, step)


def project(left_ref, w, add_ref, out_ref, shift=None, size=256):
    def step(i):
        value = dot(left_ref[...], weight_columns(w, i, size))
        if add_ref is not None:
            value = add_ref[:, at(i, size)].astype(jnp.float32) + value
        if shift is not None:
            value = value + shift[:, at(i, size)]
        out_ref[:, at(i, size)] = value.astype(out_ref.dtype)

    tiles(w.shape[2] // size, step)


def project_back(left_ref, w, out_ref, size=256):
    def step(i):
        out_ref[:, at(i, size)] = dot_nt(left_ref[...], weight_rows(w, i, size)).astype(out_ref.dtype)

    tiles(w.shape[0] * 8 // size, step)


def forward_pass(u_ref, qkv_before, bias_ref, gains, w, keep, out_ref, shift, ready, done=None, hook=None):
    done = done or (lambda *names: None)
    hook = hook or (lambda loops, count: None)
    norm_rows(u_ref, gains[0], keep["a"])
    turn(keep["a"], keep["at"])
    done("at")
    ready("qkv")
    project(keep["a"], w["qkv"], None, keep["qkv"])
    done("qkv")
    qkvs = [keep["qkv"]] if qkv_before is None else [qkv_before, keep["qkv"]]
    attend(qkvs, bias_ref, [keep["p0"], keep["p1"]], keep["rl"], keep["o"], keep["ot"], hook(6, 9))
    done("p0", "p1", "rl", "ot")
    ready("out")
    project(keep["o"], w["out"], u_ref, keep["m"])
    norm_rows(keep["m"], gains[1], keep["b"])
    turn(keep["b"], keep["bt"])
    done("m", "bt")
    ready("up")
    between = hook(12, 6)

    def step(i):
        if between is not None:
            between(i)
        hidden = dot(keep["b"][...], weight_columns(w["up"], i, 256))
        active, slope = gelu_both(hidden)
        active = active.astype(jnp.bfloat16)
        keep["f"][:, at(i, 256)] = active
        keep["ft"][at(i, 256)] = active.T
        keep["gp"][:, at(i, 256)] = slope.astype(jnp.bfloat16)

    tiles(w["up"].shape[2] // 256, step)
    done("ft", "gp")
    ready("down")
    project(keep["f"], w["down"], keep["m"], out_ref, shift)


def norm_back(u_ref, gain, dy_ref, add_ref, out_ref, rounded_ref, gain_grad_ref, sum_ref=None):
    def step(i, totals):
        total, whole = totals
        hat, spread = normal(u_ref[at(i, 128)].astype(jnp.float32))
        dy = dy_ref[at(i, 128)]
        total = total + jnp.sum((dy * hat).reshape(16, 8, dy.shape[1]), 0)
        dy = dy * gain
        down = dy - jnp.mean(dy, -1, keepdims=True) - hat * jnp.mean(dy * hat, -1, keepdims=True)
        value = add_ref[at(i, 128)].astype(jnp.float32) + spread * down
        out_ref[at(i, 128)] = value
        if rounded_ref is not None:
            rounded_ref[at(i, 128)] = value.astype(jnp.bfloat16)
        if sum_ref is not None:
            whole = whole + jnp.sum(value.reshape(16, 8, dy.shape[1]), 0)
        return total, whole

    zero = jnp.zeros((8, u_ref.shape[1]), jnp.float32)
    total, whole = lax.fori_loop(0, u_ref.shape[0] // 128, step, (zero, zero))
    gain_grad_ref[...] = jnp.broadcast_to(jnp.sum(total, 0, keepdims=True), gain_grad_ref.shape)
    if sum_ref is not None:
        sum_ref[...] = jnp.broadcast_to(jnp.sum(whole, 0, keepdims=True), sum_ref.shape)


def staged(before, count, piece, stage, sems):
    def copy(i):
        slot = lax.rem(i, 2)
        return pltpu.make_async_copy(piece(before, i), stage.at[slot], sems.at[slot])

    copy(0).start()

    def take(i):
        @pl.when(i + 1 < count)
        def _():
            copy(i + 1).start()

        copy(i).wait()
        return stage[lax.rem(i, 2)].astype(jnp.float32)

    return take


def weight_grad(turned_ref, right_ref, out_ref, before, stages, size=256):
    count = right_ref.shape[1] // size
    if before is not None:
        take = staged(before, count, lambda ref, i: ref.at[:, :, at(i, size)], stages[0], stages[2])

    def step(i):
        value = dot(turned_ref[...].astype(jnp.bfloat16), right_ref[:, at(i, size)])
        value = value.reshape(value.shape[0] // 8, 8, size)
        if before is not None:
            value = value + take(i)
        out_ref[:, :, at(i, size)] = value.astype(out_ref.dtype)

    tiles(count, step)


def turn(ref, out_ref):
    def step(i):
        out_ref[at(i, 256)] = ref[:, at(i, 256)].T

    tiles(ref.shape[1] // 256, step)


def down_grad(ft_ref, dz_ref, out_ref, before, stages, size=256):
    count = ft_ref.shape[0] // size
    if before is not None:
        take = staged(before, count, lambda ref, i: ref.at[pl.ds(i * (size // 8), size // 8)], stages[1], stages[2])

    def step(i):
        value = dot(ft_ref[at(i, size)], dz_ref[...])
        value = value.reshape(size // 8, 8, value.shape[1])
        if before is not None:
            value = value + take(i)
        out_ref[pl.ds(i * (size // 8), size // 8)] = value.astype(out_ref.dtype)

    tiles(count, step)


def backward_pass(up_ref, u_ref, qkvs, dkv_refs, gains, w, keep, work, before, stages, du_ref, gain_grads, sum_ref, ready, done, hook=None):
    before = before or dict.fromkeys(NAMES)
    dz = up_ref
    if up_ref.dtype != jnp.bfloat16:
        dz = work["dz"]

        def cast(i):
            dz[at(i, 128)] = up_ref[at(i, 128)].astype(jnp.bfloat16)

        ready("upstream")
        tiles(up_ref.shape[0] // 128, cast)
    ready("down")
    dhid = work["dhid"]

    def step(i):
        value = dot_nt(dz[...], weight_rows(w["down"], i, 256)) * keep["gp"][:, at(i, 256)].astype(jnp.float32)
        dhid[:, at(i, 256)] = value.astype(jnp.bfloat16)

    tiles(w["down"].shape[0] * 8 // 256, step)
    ready("ft")
    down_grad(keep["ft"], dz, w["down"], before["down"], stages)
    done("down")
    ready("up")
    project_back(dhid, w["up"], work["dm"])
    done("hidden")
    weight_grad(keep["bt"], dhid, w["up"], before["up"], stages)
    done("up")
    norm_back(keep["m"], gains[1], work["dm"], up_ref, work["dm"], work["da"], gain_grads[1])
    done("norm")
    ready("out")

    def head_grads(i):
        value = dot_nt(weight_rows(w["out"], i, 256), work["da"][...])
        scale = [jnp.broadcast_to(keep["rl"][2 * i + n // 2, n % 2 : n % 2 + 1], (HEAD_DIM, value.shape[1])) for n in range(4)]
        work["do"][at(i, 256)] = (value * jnp.concatenate(scale, 0)).astype(jnp.bfloat16)

    tiles(w["out"].shape[0] * 8 // 256, head_grads)
    weight_grad(keep["ot"], work["da"], w["out"], before["out"], stages)
    done("out")
    ready("attention")
    attend_back(qkvs, [keep["p0"], keep["p1"]], work["do"], keep["ot"], work["dqkv"], dkv_refs, hook)
    done("dkv")
    ready("qkv")
    project_back(work["dqkv"], w["qkv"], du_ref)
    weight_grad(keep["at"], work["dqkv"], w["qkv"], before["qkv"], stages)
    done("qkv")
    norm_back(u_ref, gains[0], du_ref, work["dm"], du_ref, None, gain_grads[0], sum_ref)


KEPT = ("at", "qkv", "rl", "ot", "m", "bt", "ft", "gp", "p0", "p1")
LOCAL = ("a", "o", "b", "f")
VMEM_LIMIT = 63 << 20
VMEM = pl.BlockSpec(memory_space=pltpu.VMEM)
FAR = pl.BlockSpec(memory_space=pl.ANY)


def shapes_of(length, model, hidden, passes):
    f32, bf16 = jnp.float32, jnp.bfloat16
    shape = jax.ShapeDtypeStruct
    pairs = model // 128
    table = {
        "a": shape((length, model), bf16),
        "at": shape((model, length), bf16),
        "qkv": shape((length, 3 * model), bf16),
        "rl": shape((pairs, 2, length), f32),
        "o": shape((length, model), bf16),
        "ot": shape((model, length), f32),
        "m": shape((length, model), f32),
        "b": shape((length, model), bf16),
        "bt": shape((model, length), bf16),
        "f": shape((length, hidden), bf16),
        "ft": shape((hidden, length), bf16),
        "gp": shape((length, hidden), bf16),
        "dz": shape((length, model), bf16),
        "do": shape((model, length), bf16),
        "dm": shape((length, model), f32),
        "dqkv": shape((length, 3 * model), bf16),
        "dkv": shape((length, 2 * model), f32),
        "bias": shape((length, length), f32),
        "u": shape((length, model), f32),
        "vectors": shape((8, model), f32),
    }
    for b in range(length // QB):
        table["p%d" % b] = shape((pairs, 2, passes * (b + 1) * QB, QB), bf16)
    return table


class Room:
    def __init__(self):
        self.names, self.shapes, self.moves = [], [], []

    def scratch(self, **shapes):
        for name, s in shapes.items():
            self.names.append(name)
            self.shapes.append(pltpu.VMEM(s.shape, s.dtype))

    def bind(self, refs):
        return dict(zip(self.names, refs))


class Mover:
    def __init__(self, sems):
        self.sems, self.open, self.used = sems, {}, 0

    def start(self, src, dst, key):
        copy = pltpu.make_async_copy(src, dst, self.sems.at[self.used])
        self.used += 1
        copy.start()
        self.open[key] = copy

    def wait(self, *keys):
        for key in keys:
            if key in self.open:
                self.open.pop(key).wait()

    def close(self):
        self.wait(*list(self.open))


def make_bias(docs, bias_ref):
    length = bias_ref.shape[0]
    down = jnp.broadcast_to(docs[...], (128, length)).T

    def step(i):
        place_down = lax.broadcasted_iota(jnp.int32, (length, 128), 0)
        place_across = lax.broadcasted_iota(jnp.int32, (length, 128), 1) + i * 128
        seen = (down == docs[:, at(i, 128)]) & (place_down <= place_across)
        bias_ref[:, at(i, 128)] = jnp.where(seen, 0.0, -1e30)

    tiles(length // 128, step)


def spread_vectors(small, vectors_ref, rows):
    count, model = small.shape[0], vectors_ref.shape[1]
    lane = lax.broadcasted_iota(jnp.int32, (128, model), 1)
    place = lax.broadcasted_iota(jnp.int32, (128, model), 0)
    block = (lane * 2731) >> 16
    pick = jnp.where(lane - block * rows == place, 1.0, 0.0).astype(jnp.bfloat16)
    wide = dot(small[...].reshape(count * 8, 128), pick)
    row = lax.broadcasted_iota(jnp.int32, wide.shape, 0)
    owner = (lax.broadcasted_iota(jnp.int32, wide.shape, 1) * 2731) >> 16
    wide = jnp.where((row >> 3) == owner, wide, 0.0)
    vectors_ref[...] = jnp.sum(wide.reshape(count, 8, model), 0)


def gather_chunks(weights):
    chunks = [("small", ((0, 128),))]
    for name, parts in (("out", 1), ("qkv", 3), ("up", 2), ("down", 2)):
        chunks += [(name, halves) for halves in pieces(weights[name].shape[2], parts)]
    return chunks


def first_kernel(near, table, room, chunks, *refs):
    it = iter(refs)
    tokens, docs = next(it), next(it)
    shards = {n: next(it) for n in NAMES}
    if near:
        shards["small"] = next(it)
    else:
        vectors = next(it)
    far = {n: next(it) for n in ("u",) + KEPT}
    if near:
        whole = {n: next(it) for n in NAMES}
        vectors = next(it)
    refs = list(it)
    v = room.bind(refs)
    sems = refs[len(room.names) :]
    mover = Mover(sems[0])
    w = {n: v["w_" + n] for n in NAMES}
    pump = None
    if near:
        gather = Gather(chunks, shards, {**w, "small": v["small"]}, sems[1:])
        pump = Pump(gather.step, staggered(len(chunks), 2, ("first", "second", "third", "fourth", "finish")))
        gather.links.greet()
        for one in pump.take(2):
            pump.run(*one)
    else:
        for n in NAMES:
            mover.start(shards[n], w[n], "w_" + n)
    make_bias(docs, v["bias"])
    if near:
        pump.until("finish", 0)
        spread_vectors(v["small"], vectors, 24)
    last = {name: n for n, (name, _) in enumerate(chunks)}

    def ready(name):
        if near:
            pump.until("finish", last[name])
            mover.start(w[name], whole[name], "whole_" + name)
        else:
            mover.wait("w_" + name)

    def hook(loops, count):
        return pump.hook(loops, count) if near else None

    def done(*names):
        for n in names:
            mover.start(v[n], far[n], "far_" + n)

    gains = [vectors[n : n + 1] for n in (1, 2)]
    forward_pass(tokens, None, v["bias"], gains, w, v, v["u"], vectors.at[0:1], ready, done, hook)
    mover.start(v["u"], far["u"], "far_u")
    if near:
        pump.rest()
        for n in range(len(chunks)):
            gather.step("close", n)
    mover.close()


def run_first(near, tokens, docs, small, vectors, shards):
    length, model = tokens.shape
    devices = 32 if near else 1
    weights = {n: jax.ShapeDtypeStruct((devices * s.shape[0],) + s.shape[1:], s.dtype) for n, s in shards.items()}
    table = shapes_of(length, model, weights["up"].shape[2], 1)
    room = Room()
    room.scratch(**{n: table[n] for n in KEPT + LOCAL + ("bias", "u")}, **{"w_" + n: weights[n] for n in NAMES})
    chunks = gather_chunks(weights) if near else []
    out_shape = [table[n] for n in ("u",) + KEPT]
    semaphores = [pltpu.SemaphoreType.DMA((24,))]
    params = dict(vmem_limit_bytes=VMEM_LIMIT)
    out_specs = [FAR] * len(out_shape)
    inputs = [tokens, docs] + [shards[n] for n in NAMES]
    if near:
        room.scratch(small=jax.ShapeDtypeStruct((32, 8, 128), jnp.bfloat16))
        out_shape += [weights[n] for n in NAMES] + [table["vectors"]]
        out_specs += [FAR] * 4 + [VMEM]
        semaphores += link_semaphores(len(chunks))
        params.update(collective_id=0, has_side_effects=True)
        inputs, in_specs = inputs + [small], [VMEM] * 2 + [FAR] * 5
    else:
        inputs, in_specs = inputs + [vectors], [VMEM] * 2 + [FAR] * 4 + [VMEM]
    outs = pl.pallas_call(
        functools.partial(first_kernel, near, table, room, chunks),
        out_shape=out_shape,
        in_specs=in_specs,
        out_specs=out_specs,
        scratch_shapes=room.shapes + semaphores,
        name="first",
        compiler_params=pltpu.CompilerParams(**params),
    )(*inputs)
    kept = dict(zip(("u",) + KEPT, outs))
    if near:
        return kept, outs[-1], dict(zip(NAMES, outs[1 + len(KEPT) :]))
    return kept, vectors, shards


def middle_kernel(table, room, *refs):
    it = iter(refs)
    u, docs, vectors = next(it), next(it), next(it)
    cotangent, qkv_before = next(it), next(it)
    weights = {n: next(it) for n in NAMES}
    ln1, ln2, whole = next(it), next(it), next(it)
    layer_out, du, dkv = next(it), next(it), next(it)
    grads = {n: next(it) for n in NAMES}
    refs = list(it)
    v = room.bind(refs)
    mover = Mover(refs[len(room.names)])
    w = {n: v["w_" + n] for n in NAMES}
    mover.start(weights["qkv"], w["qkv"], "w_qkv")
    mover.start(qkv_before, v["before"], "before")
    for n in NAMES[1:]:
        mover.start(weights[n], w[n], "w_" + n)
    mover.start(cotangent, v["dz"], "dz")
    make_bias(docs, v["bias"])
    gains = [vectors[n : n + 1] for n in (1, 2)]

    def ready(name):
        if name == "qkv":
            mover.wait("before")
        mover.wait("w_" + name)

    forward_pass(u, v["before"], v["bias"], gains, w, v, v["b"], None, ready)
    mover.start(v["b"], layer_out, "layer_out")
    mover.wait("dz")
    work = dict(dz=v["dz"], da=v["a"], do=v["do"], dm=v["dm"], dhid=v["f"], dqkv=v["dqkv"], du=v["m"])

    def done(name):
        if name == "dkv":
            mover.start(v["dkv"], dkv, "dkv")
        elif name in NAMES:
            mover.start(w[name], grads[name], "g_" + name)

    backward_pass(
        v["dz"], u, [v["before"], v["qkv"]], [v["dkv"], None], gains, w, v, work, None, None, v["m"], (ln1, ln2), whole, no_wait, done
    )
    mover.start(v["m"], du, "du")
    mover.close()


def no_wait(name):
    pass


def run_middle(u, docs, vectors, cotangent, qkv_before, weights):
    length, model = u.shape
    table = shapes_of(length, model, weights["up"].shape[2], 2)
    room = Room()
    room.scratch(**{n: table[n] for n in KEPT + LOCAL + ("bias", "dz", "do", "dm", "dqkv", "dkv")}, before=table["qkv"])
    room.scratch(**{"w_" + n: weights[n] for n in NAMES})
    out_shape = [table["vectors"]] * 3 + [table["b"], table["u"], table["dkv"]] + [weights[n] for n in NAMES]
    outs = pl.pallas_call(
        functools.partial(middle_kernel, table, room),
        out_shape=out_shape,
        in_specs=[VMEM] * 3 + [FAR] * 6,
        out_specs=[VMEM] * 3 + [FAR] * 7,
        scratch_shapes=room.shapes + [pltpu.SemaphoreType.DMA((16,))],
        name="middle",
        compiler_params=pltpu.CompilerParams(vmem_limit_bytes=VMEM_LIMIT),
    )(u, docs, vectors, cotangent, qkv_before, *(weights[n] for n in NAMES))
    return outs[:3], outs[3], outs[4], outs[5], dict(zip(NAMES, outs[6:]))


LATE = {
    "down": [("begin", 0), ("begin", 1)],
    "hidden": [("first", 0)],
    "up": [("begin", 2), ("begin", 3), ("first", 1)],
    "norm": [("second", 0), ("first", 2)],
    "out": [("begin", 4), ("second", 1), ("first", 3)],
}
INSIDE = [
    [("third", 0), ("second", 2)],
    [("third", 1), ("first", 4)],
    [("finish", 0), ("second", 3)],
    [("third", 2), ("finish", 1)],
    [("second", 4), ("third", 3)],
    [("finish", 2)],
]
AFTER = [("begin", 5), ("begin", 6), ("begin", 7), ("third", 4), ("finish", 3), ("first", 5)]
TAIL = [
    ("begin", 8), ("first", 6), ("second", 5), ("first", 7), ("second", 6), ("third", 5), ("finish", 4), ("first", 8), ("second", 7),
    ("third", 6), ("second", 8), ("finish", 5), ("third", 7), ("third", 8), ("finish", 6), ("finish", 7), ("finish", 8),
]


def reduce_chunks(weights):
    chunks = []
    for name, parts in (("down", 2), ("up", 2), ("out", 1), ("qkv", 3)):
        chunks += [(name, halves) for halves in pieces(weights[name].shape[2], parts)]
    return chunks + [("small", ((0, 128),))]


def fold_vectors(vector, small, rows):
    count, model = small.shape[0], vector.shape[1]
    lane = lax.broadcasted_iota(jnp.int32, (128, model), 1)
    place = lax.broadcasted_iota(jnp.int32, (128, model), 0)
    block = (lane * 2731) >> 16
    pick = jnp.where(lane - block * rows == place, 1.0, 0.0).astype(jnp.bfloat16)
    wide = jnp.broadcast_to(vector[None], (count, 8, model)).reshape(count * 8, model)
    row = lax.broadcasted_iota(jnp.int32, wide.shape, 0)
    owner = (lax.broadcasted_iota(jnp.int32, wide.shape, 1) * 2731) >> 16
    wide = jnp.where((row >> 3) == owner, wide, 0.0).astype(jnp.bfloat16)
    small[...] = dot_nt(wide, pick).astype(jnp.bfloat16).reshape(small.shape)


def last_kernel(near, room, chunks, *refs):
    it = iter(refs)
    tokens, vectors, late1, late2, embed = next(it), next(it), next(it), next(it), next(it)
    far = {n: next(it) for n in ("upstream", "dkv") + KEPT}
    weights = {n: next(it) for n in NAMES}
    before = {n: next(it) for n in NAMES}
    du = next(it)
    outs = {n: next(it) for n in NAMES + ("small",)}
    refs = list(it)
    v = room.bind(refs)
    sems = refs[len(room.names) :]
    mover = Mover(sems[0])
    w = {n: v["w_" + n] for n in NAMES}
    mover.start(far["upstream"], v["upstream"], "upstream")
    mover.start(weights["down"], w["down"], "w_down")
    for n in ("gp", "ft"):
        mover.start(far[n], v[n], n)
    mover.start(weights["up"], w["up"], "w_up")
    for n in ("bt", "m"):
        mover.start(far[n], v[n], n)
    mover.start(weights["out"], w["out"], "w_out")
    for n in ("rl", "ot", "qkv", "p0", "p1", "dkv"):
        mover.start(far[n], v[n], n)
    mover.start(weights["qkv"], w["qkv"], "w_qkv")
    mover.start(far["at"], v["at"], "at")
    needs = {
        "upstream": ("upstream",),
        "down": ("w_down", "gp"),
        "ft": ("ft",),
        "up": ("w_up", "bt", "m"),
        "out": ("w_out", "rl", "ot"),
        "attention": ("qkv", "p0", "p1", "dkv"),
        "qkv": ("w_qkv", "at"),
    }

    def ready(name):
        mover.wait(*needs[name])

    hook = None
    if near:
        reduce = Reduce(
            chunks, {**w, "small": v["small"]}, *({n: v["r%d_%s" % (k, n)] for n in NAMES + ("small",)} for k in range(4)), outs, sems[2:]
        )
        reduce.links.greet()

        def run(events):
            for what, n in events:
                reduce.step(what, n)

        def hook(pair):
            for k, events in enumerate(INSIDE):

                @pl.when(pair == k)
                def _(events=events):
                    run(events)

    def done(name):
        if near:
            run(LATE.get(name, ()))
            if name == "qkv":
                run(AFTER)
        elif name in NAMES:
            mover.start(w[name], outs[name], "g_" + name)

    work = dict(dz=v["dz"], da=v["dz"], do=v["do"], dm=v["dm"], dhid=v["gp"], dqkv=v["dqkv"])
    gains = [vectors[n : n + 1] for n in (1, 2)]
    backward_pass(
        v["upstream"], tokens, [v["qkv"]], [v["dkv"]], gains, w, v, work, before, (v["stage0"], v["stage1"], sems[1]),
        v["m"], (v["ln1"], v["ln2"]), None, ready, done, hook,
    )
    mover.start(v["m"], du, "du")
    row = lax.broadcasted_iota(jnp.int32, embed.shape, 0)
    vector = jnp.where(row == 0, embed[...], jnp.where(row == 1, late1[...] + v["ln1"][...], jnp.where(row == 2, late2[...] + v["ln2"][...], 0.0)))
    if near:
        fold_vectors(vector, v["small"], 24)
        run(TAIL)
        for n in range(len(chunks)):
            reduce.step("close", n)
    else:
        outs["small"][...] = vector
    mover.close()


def run_last(near, tokens, vectors, late1, late2, embed, upstream, dkv, kept, weights, before):
    length, model = tokens.shape
    bf16 = jnp.bfloat16
    shape = jax.ShapeDtypeStruct
    table = shapes_of(length, model, weights["up"].shape[2], 1)
    room = Room()
    room.scratch(**{n: table[n] for n in KEPT + ("dz", "do", "dm", "dqkv", "dkv")}, upstream=table["u"])
    room.scratch(ln1=table["vectors"], ln2=table["vectors"])
    room.scratch(**{"w_" + n: weights[n] for n in NAMES})
    room.scratch(stage0=shape((2, model // 8, 8, 256), bf16), stage1=shape((2, 32, 8, model), bf16))
    chunks = reduce_chunks(weights) if near else []
    semaphores = [pltpu.SemaphoreType.DMA((24,)), pltpu.SemaphoreType.DMA((2,))]
    params = dict(vmem_limit_bytes=VMEM_LIMIT)
    if near:
        parts = {**weights, "small": shape((32, 8, 128), bf16)}
        room.scratch(small=parts["small"])
        for k, blocks in enumerate((16, 8, 4, 3)):
            room.scratch(**{"r%d_%s" % (k, n): shape((p.shape[0] // 32 * blocks,) + p.shape[1:], bf16) for n, p in parts.items()})
        out_shape = [shape((parts[n].shape[0] // 32,) + parts[n].shape[1:], jnp.float32) for n in NAMES + ("small",)]
        out_specs = [VMEM] * 5
        semaphores += link_semaphores(len(chunks))
        params.update(collective_id=1, has_side_effects=True)
    else:
        out_shape = [weights[n] for n in NAMES] + [table["vectors"]]
        out_specs = [FAR] * 4 + [VMEM]
    outs = pl.pallas_call(
        functools.partial(last_kernel, near, room, chunks),
        out_shape=[table["u"]] + out_shape,
        in_specs=[VMEM] * 5 + [FAR] * (2 + len(KEPT) + 8),
        out_specs=[FAR] + out_specs,
        scratch_shapes=room.shapes + semaphores,
        name="last",
        compiler_params=pltpu.CompilerParams(**params),
    )(tokens, vectors, late1, late2, embed, upstream, dkv, *(kept[n] for n in KEPT), *(weights[n] for n in NAMES), *(before[n] for n in NAMES))
    return outs[0], dict(zip(NAMES, outs[1:])), outs[5]


AXES = ("dp", "fsdp")


def cut(w):
    return w.reshape(w.shape[0] // 8, 8, w.shape[1])


def join(w):
    return w.reshape(w.shape[0] * 8, w.shape[2])


def body(near, tokens, doc_ids, pass_embed, ln1_gain, w_qkv, w_out, ln2_gain, w_up, w_down, cotangent):
    shards = {"qkv": w_qkv, "out": w_out, "up": w_up, "down": w_down}
    docs = doc_ids.astype(jnp.float32).reshape(1, -1)
    rows = pass_embed.shape[0]
    small = vectors = None
    if near:
        small = jnp.zeros((1, 8, 128), jnp.bfloat16).at[0, :3, :rows].set(jnp.stack([pass_embed, ln1_gain, ln2_gain]))
        shards = {n: cut(s) for n, s in shards.items()}
    else:
        vectors = jnp.stack([lax.all_gather(v, AXES, axis=0, tiled=True) for v in (pass_embed, ln1_gain, ln2_gain)])
        vectors = jnp.pad(vectors.astype(jnp.float32), ((0, 5), (0, 0)))
        shards = {n: cut(lax.all_gather(s, AXES, axis=0, tiled=True)) for n, s in shards.items()}
    kept, vectors, weights = run_first(near, tokens, docs, small, vectors, shards)
    (late1, late2, embed), layer_out, second_g, dkv, late = run_middle(kept["u"], docs, vectors, cotangent, kept["qkv"], weights)
    tokens_grad, sums, small = run_last(near, tokens, vectors, late1, late2, embed, second_g, dkv, kept, weights, late)
    if near:
        sums = {n: join(s) for n, s in sums.items()}
        small = [small[0, n, :rows] for n in range(3)]
    else:
        scatter = lambda v: lax.psum_scatter(v, AXES, scatter_dimension=0, tiled=True)
        sums = {n: scatter(join(s).astype(jnp.float32)) for n, s in sums.items()}
        small = [scatter(small[n]) for n in range(3)]
    return (layer_out, tokens_grad, small[0], small[1], sums["qkv"], sums["out"], small[2], sums["up"], sums["down"])


def solution(mesh):
    near = dict(mesh.shape) == {"dp": 8, "fsdp": 4}
    placed = (
        P(("dp", "fsdp"), None),
        P(("dp", "fsdp")),
        P(("dp", "fsdp")),
        P(("dp", "fsdp")),
        P(("dp", "fsdp"), None),
        P(("dp", "fsdp"), None),
        P(("dp", "fsdp")),
        P(("dp", "fsdp"), None),
        P(("dp", "fsdp"), None),
        P(("dp", "fsdp"), None),
    )
    return jax.shard_map(
        functools.partial(body, near),
        mesh=mesh,
        in_specs=placed,
        out_specs=(
            P(("dp", "fsdp"), None),
            P(("dp", "fsdp"), None),
            P(("dp", "fsdp")),
            P(("dp", "fsdp")),
            P(("dp", "fsdp"), None),
            P(("dp", "fsdp"), None),
            P(("dp", "fsdp")),
            P(("dp", "fsdp"), None),
            P(("dp", "fsdp"), None),
        ),
        check_vma=False,
    )
```

time: 384 us -> 296 us (0.77)
  Pallas kernels: 368 us -> 285 us
    pallas_call x6 -> x3, Pallas kernels: 368 us -> 285 us  [the longest x1 112 us: run_last(): pl.pallas_call(functools.partial(last_kernel, near, room, chunks), out_sh...]
where the time goes in v3:
time: 296 us; the launch traced here: 295 us
  Pallas kernels  285 us (96%)
  local copies, waits for them, and re-layouts  7.31 us (2%)
    pallas_call x1, Pallas kernels, run_last(): pl.pallas_call(functools.partial(last_kernel, near, room, chunks), out_sh...  112 us
    pallas_call x1, Pallas kernels, run_first(): pl.pallas_call(functools.partial(first_kernel, near, table, room, chunks)...  95.2 us
    pallas_call x1, Pallas kernels, run_middle(): pl.pallas_call(functools.partial(middle_kernel, table, room), out_shape=o...  78.5 us

profile of v3, /device:TPU:0, one launch (start us, length us, event | category | flops | bytes accessed | tf_op | source)
XLA Modules:
  0.0 295.2 jit_solution(12888399611034083968)
XLA Ops:
  0.6 1.3 convert_element_type.3
  1.9 0.7 maximum_bitcast_fusion
  2.6 0.6 scatter.4.refs_6_
  3.2 95.2 %first.1 = (f32[512,768]{1,0:T(8,128)}, bf16[768,512]{1,0:T(8,128)(2,1)}, bf16[512,2304]{1,0:T(8,128)(2,1)}, f32[6,2,512]{2,1,0:T(2,128)}, f32[768,512]{1,0:T(8,...) custom-call(bf16[512,768]{1,0:T(8,128)(2,1)} %refs_0_.3, ...), custom_call_target="tpu_custom_call" | custom-call | tf_op jit(solution)/shard_map/first/pallas_call | solution.py:819
  98.4 78.5 %middle.1 = (f32[8,768]{1,0:T(8,128)}, f32[8,768]{1,0:T(8,128)}, f32[8,768]{1,0:T(8,128)}, bf16[512,768]{1,0:T(8,128)(2,1)}, f32[512,768]{1,0:T(8,128)}, /*index...) custom-call(f32[512,768]{1,0:T(8,128)} %get-tuple-element.53.refs_0_, ...), custom_call_target="tpu_custom_call" | custom-call | tf_op jit(solution)/shard_map/middle/pallas_call | solution.py:888
  176.9 111.5 %last.1 = (f32[512,768]{1,0:T(8,128)}, f32[3,8,2304]{2,1,0:T(8,128)}, f32[3,8,768]{2,1,0:T(8,128)}, f32[3,8,3072]{2,1,0:T(8,128)}, f32[12,8,768]{2,1,0:T(8,128)}, /*index=5*/f32[1,8,128]{2,1,0:T(8,128)}) custom-call(bf16[512,768]{1,0:T(8,128)(2,1)} %refs_0_.3, f32[8,768]{1,0:T(8,128)} %get-tuple-element.54.refs_2_.refs_1_, ...), custom_call_target="tpu_custom_call" | custom-call | tf_op jit(solution)/shard_map/last/pallas_call | solution.py:1050
  288.4 0.0 copy-start.2
  288.4 0.0 copy-start.3
  288.4 0.0 copy-start.1
  288.4 0.0 copy-start
  288.5 1.3 slice_bitcast_fusion
  289.8 2.7 copy.24
  292.4 0.0 copy-done.2
  292.4 0.7 copy.25
  293.1 0.0 copy-done.3
  293.1 0.6 copy.26
  293.7 0.0 copy-done.1
  293.7 0.7 copy.27
  294.5 0.0 copy-done
  294.5 0.7 copy.28
Async XLA Ops:
  288.4 4.0 %copy-start.2 = (f32[3,8,2304]{2,1,0:T(8,128)S(1)}, f32[3,8,2304]{2,1,0:T(8,128)}, u32[]{:S(2)}) copy-start(f32[3,8,2304]{2,1,0:T(8,128)} %get-tuple-element.81) | copy-start | bytes 663556
  288.4 4.7 %copy-start.3 = (f32[3,8,768]{2,1,0:T(8,128)S(1)}, f32[3,8,768]{2,1,0:T(8,128)}, u32[]{:S(2)}) copy-start(f32[3,8,768]{2,1,0:T(8,128)} %get-tuple-element.82) | copy-start | bytes 221188
  288.4 5.3 %copy-start.1 = (f32[3,8,3072]{2,1,0:T(8,128)S(1)}, f32[3,8,3072]{2,1,0:T(8,128)}, u32[]{:S(2)}) copy-start(f32[3,8,3072]{2,1,0:T(8,128)} %get-tuple-element.83) | copy-start | bytes 884740
  288.4 6.0 %copy-start = (f32[12,8,768]{2,1,0:T(8,128)S(1)}, f32[12,8,768]{2,1,0:T(8,128)}, u32[]{:S(2)}) copy-start(f32[12,8,768]{2,1,0:T(8,128)} %get-tuple-element.84) | copy-start | bytes 884740
